TPU v7x, 256 devices: a whole 4x4x8 slice. The times are simulated.
256 devices in a mesh: panel: 2 (over y_hi), colat: 8 (over x, core), lon: 16 (over z, y_lo).
Axes of the slice: x: 4, y: 4 (y_hi: 2, y_lo: 2; y = y_hi * 2 + y_lo), z: 8, core: 2. Of those that a mesh axis runs over, the one named last changes fastest.
Arguments:
- state: float32 [2, 7, 256, 16384], P('panel', None, 'colat', 'lon'), may hold values from -6 to 6
- spin: float32 [2, 256, 512], P('panel', 'colat', 'lon'), may hold values from -1 to 1
- donor_device: int32 [4, 1536], replicated, may hold values from 0 to 127, as said below
- donor_row: int32 [4, 1536], replicated, may hold values from 0 to 31, as said below
- donor_col: int32 [4, 1536], replicated, may hold values from 0 to 31, as said below
- corner_weights: float32 [4, 1536], replicated, may hold values from 0 to 1, as said below
- border_angle: float32 [1536], replicated, may hold values from -3.8 to 3.8, as said below
Outputs:
- advanced: float32 [2, 7, 256, 16384], P('panel', None, 'colat', 'lon')
Inputs may be any that keep to these rules, and one draw needn't show every extreme that they name: `donor_device`: devices of a panel are numbered colatitude block * 16 + longitude block. The four corners c = 0, 1, 2, 3 of a border point are the cells (i, j), (i+1, j), (i, j+1), (i+1, j+1) of one square of the other panel, never in that panel's border rows or columns. `donor_row`: local row of the corner named by donor_device. `donor_col`: local column of the corner named by donor_device. `corner_weights`: bilinear weights: the four of a border point are products of (1 - a or a) and (1 - s or s) and sum to one. `border_angle`: angle in radians.
All inputs are finite; a program needn't handle non-finite values.
Results may differ from a plain program's by a relative error of at most 0.00016.
Values sent between devices are 32-bit elements; how exact they have to be, the bound alone decides.
A program may use at most 64 MiB of HBM per device.

v0:
```python
import jax
import jax.numpy as jnp
from jax import lax
from jax.sharding import PartitionSpec as P

FIELDS = 7
NR = 32


viscosity = 0.3
conduction = 0.4
resistance = 0.5
buoyancy = 1.0
timestep = 0.2


def with_halo(block, sides, width):
    for axis, dim in sides:
        count = lax.axis_size(axis)
        forward = [(i, i + 1) for i in range(count - 1)]
        backward = [(target, source) for source, target in forward]
        low = lax.ppermute(
            lax.slice_in_dim(block, block.shape[dim] - width, None, axis=dim), axis, forward
        )
        high = lax.ppermute(lax.slice_in_dim(block, 0, width, axis=dim), axis, backward)
        block = jnp.concatenate([low, block, high], axis=dim)
    return block


def partner(value, axis, distance):
    mask = 2**distance
    pairs = [(source, source ^ mask) for source in range(lax.axis_size(axis))]
    return lax.ppermute(value, axis, pairs)


def field_rates(
    fields,
    north_cells,
    south_cells,
    west_cells,
    east_cells,
    upper_cells,
    lower_cells,
    metric_t,
    metric_p,
    spin_cells,
):
    colat_slope = metric_t * (0.5 * (south_cells - north_cells))
    lon_slope = metric_p * (0.5 * (east_cells - west_cells))
    radial_slope = 0.5 * (upper_cells - lower_cells)
    laplace = (
        metric_t * metric_t * (south_cells + north_cells - 2.0 * fields)
        + metric_p * metric_p * (east_cells + west_cells - 2.0 * fields)
        + (upper_cells + lower_cells - 2.0 * fields)
    )
    advected = fields[0] * colat_slope + fields[1] * lon_slope + fields[2] * radial_slope
    stretched = fields[4] * colat_slope + fields[5] * lon_slope + fields[6] * radial_slope
    diffuse_rate = jnp.array(
        [viscosity, viscosity, viscosity, conduction, resistance, resistance, resistance],
        jnp.float32,
    )
    diffuse_rate = diffuse_rate.reshape((7,) + (1,) * (fields.ndim - 1))
    base_rate = diffuse_rate * laplace - advected
    return jnp.stack(
        [
            base_rate[0] + stretched[4] + spin_cells * fields[1],
            base_rate[1] + stretched[5] - spin_cells * fields[0],
            base_rate[2] + stretched[6] + buoyancy * fields[3],
            base_rate[3],
            base_rate[4] + stretched[0],
            base_rate[5] + stretched[1],
            base_rate[6] + stretched[2],
        ]
    )


def slot_map(colat_block, lon_block, lat_rows, lon_cells, n_colat, n_lon):
    slot_count = 2 * (lat_rows + lon_cells)
    lat_total = lat_rows * n_colat
    lon_total = lon_cells * n_lon
    slot_ids = jnp.arange(slot_count, dtype=jnp.int32)[None, :]
    colat_block = colat_block[:, None]
    lon_block = lon_block[:, None]
    is_top = slot_ids < lon_cells
    is_bottom = (slot_ids >= lon_cells) & (slot_ids < 2 * lon_cells)
    is_left = (slot_ids >= 2 * lon_cells) & (slot_ids < 2 * lon_cells + lat_rows)
    along_lon = lon_block * lon_cells + slot_ids
    along_lat = colat_block * lat_rows + slot_ids - 2 * lon_cells
    index_map = jnp.where(
        is_top,
        along_lon,
        jnp.where(
            is_bottom,
            lon_total + along_lon - lon_cells,
            jnp.where(
                is_left, 2 * lon_total + along_lat, 2 * lon_total + lat_total + along_lat - lat_rows
            ),
        ),
    )
    return index_map


def on_device(state, spin, donor_device, donor_row, donor_col, corner_weights, border_angle):
    fields = state[0]
    lat_rows = fields.shape[1]
    width = fields.shape[2]
    lon_cells = width // NR
    n_colat = lax.axis_size("colat")
    n_lon = lax.axis_size("lon")
    colat_block = lax.axis_index("colat")
    lon_block = lax.axis_index("lon")
    shell_index = jnp.arange(width, dtype=jnp.int32) % NR
    shell_float = shell_index.astype(jnp.float32)
    inv_radius = 1.0 / (1.0 + 0.25 * (shell_float + 0.5) / NR)
    row_number = (colat_block * lat_rows + jnp.arange(lat_rows, dtype=jnp.int32)).astype(
        jnp.float32
    )
    colat_angle = jnp.pi / 4 + (row_number + 0.5) * (jnp.pi / (2.0 * (lat_rows * n_colat)))
    metric_p = inv_radius[None, :] / jnp.sin(colat_angle)[:, None]
    spin_cells = jnp.repeat(spin[0], NR, axis=1)
    own_slots = slot_map(
        jnp.reshape(colat_block, (1,)),
        jnp.reshape(lon_block, (1,)),
        lat_rows,
        lon_cells,
        n_colat,
        n_lon,
    )[0]
    slot_angle = jnp.take(border_angle, own_slots)
    cosine = jnp.cos(slot_angle)
    sine_part = jnp.sin(slot_angle)
    cell_index = donor_row * lon_cells + donor_col
    is_mine = donor_device == colat_block * n_lon + lon_block
    per_device = FIELDS * NR

    def tendency(current):
        colat_ext = with_halo(current, (("colat", 1),), 1)
        lon_ext = with_halo(current, (("lon", 2),), NR)
        north_cells = colat_ext[:, :-2]
        south_cells = colat_ext[:, 2:]
        west_cells = lon_ext[:, :, : -2 * NR]
        east_cells = lon_ext[:, :, 2 * NR :]
        upper_cells = jnp.where(
            shell_index == NR - 1,
            current,
            jnp.concatenate([current[..., 1:], current[..., -1:]], axis=-1),
        )
        lower_cells = jnp.where(
            shell_index == 0,
            current,
            jnp.concatenate([current[..., :1], current[..., :-1]], axis=-1),
        )
        return field_rates(
            current,
            north_cells,
            south_cells,
            west_cells,
            east_cells,
            upper_cells,
            lower_cells,
            inv_radius,
            metric_p,
            spin_cells,
        )

    def border_terms_of(source):
        flat_block = (
            source.reshape(FIELDS, lat_rows, lon_cells, NR)
            .transpose(0, 3, 1, 2)
            .reshape(per_device, lat_rows * lon_cells)
        )
        summed = jnp.zeros((per_device, donor_row.shape[1]), jnp.float32)
        for corner in range(4):
            weight = jnp.where(is_mine[corner], corner_weights[corner], 0.0)
            summed = summed + jnp.take(flat_block, cell_index[corner], axis=1) * weight[None, :]
        return summed

    def rotate(picked):
        return jnp.stack(
            [
                cosine * picked[0] - sine_part * picked[1],
                sine_part * picked[0] + cosine * picked[1],
                picked[2],
                picked[3],
                cosine * picked[4] - sine_part * picked[5],
                sine_part * picked[4] + cosine * picked[5],
                picked[6],
            ]
        )

    def place_border(target, turned):
        top_row = turned[:, :, 0:lon_cells].transpose(0, 2, 1).reshape(FIELDS, width)
        bottom_row = (
            turned[:, :, lon_cells : 2 * lon_cells].transpose(0, 2, 1).reshape(FIELDS, width)
        )
        left_col = turned[:, :, 2 * lon_cells : 2 * lon_cells + lat_rows].transpose(0, 2, 1)
        right_col = turned[:, :, 2 * lon_cells + lat_rows :].transpose(0, 2, 1)
        target = target.at[:, 0, :].set(jnp.where(colat_block == 0, top_row, target[:, 0, :]))
        target = target.at[:, lat_rows - 1, :].set(
            jnp.where(colat_block == n_colat - 1, bottom_row, target[:, lat_rows - 1, :])
        )
        row_ids = jnp.arange(lat_rows)
        edge_row = (row_ids == 0) & (colat_block == 0) | (row_ids == lat_rows - 1) & (
            colat_block == n_colat - 1
        )
        current = target[:, :, 0:NR]
        blended = jnp.where(edge_row[None, :, None], 0.5 * (left_col + current), left_col)
        target = target.at[:, :, 0:NR].set(jnp.where(lon_block == 0, blended, current))
        current = target[:, :, width - NR :]
        blended = jnp.where(edge_row[None, :, None], 0.5 * (right_col + current), right_col)
        target = target.at[:, :, width - NR :].set(
            jnp.where(lon_block == n_lon - 1, blended, current)
        )
        return target

    def overset(target):
        source = partner(target, "panel", 0)
        summed_all = lax.psum(border_terms_of(source), ("colat", "lon"))
        picked = jnp.take(summed_all, own_slots, axis=1)
        turned = rotate(picked.reshape(FIELDS, NR, -1))
        return place_border(target, turned)

    tendency_now = tendency(fields)
    middle = overset(fields + 0.5 * timestep * tendency_now)
    tendency_now = tendency(middle)
    advanced = overset(fields + timestep * tendency_now)
    return advanced[None]


def solution(mesh):
    placed = (P("panel", None, "colat", "lon"), P("panel", "colat", "lon"), P(), P(), P(), P(), P())
    return jax.shard_map(
        on_device,
        mesh=mesh,
        in_specs=placed,
        out_specs=P("panel", None, "colat", "lon"),
        check_vma=False,
    )
```

profile of v0, /device:TPU:1, one launch (start us, length us, event | category | flops | bytes accessed | tf_op | source)
XLA Modules:
  0.0 2294.5 jit_solution(10925079647224834727)
XLA Ops:
  9.5 5.3 collective-permute-start.3
  16.6 5.0 collective-permute-start
  36.4 2.5 collective-permute-start.4
  39.2 19.7 collective-permute-done.4
  58.9 2.5 reshape.619
  61.5 7.3 copy.189
  68.8 3.3 reshape.745
  72.1 4.6 gather_fusion.1
  76.8 4.7 gather_fusion.2
  81.4 4.6 gather_fusion.3
  86.1 4.6 gather_fusion.4
  90.8 6.3 fusion.3
  98.6 1047.4 %all-reduce.3.cloned.1.call-done = f32[224,1536]{0,1:T(8,128)} async-done(((f32[224,1536]{0,1:T(8,128)}), f32[224,1536]{0,1:T(8,128)}) %all-reduce.3.cloned.1.call-update) | async-done | bytes 1376272 | tf_op jit(solution)/shard_map/psum | solution.py:218
  1154.8 6.9 collective-permute-start.5
  1170.7 20.6 collective-permute-done.9
  1191.3 2.5 reshape.623
  1193.9 7.3 copy.191
  1201.2 3.3 reshape.748
  1204.5 3.7 gather_fusion.6
  1208.2 4.6 gather_fusion.7
  1212.9 4.7 gather_fusion.8
  1217.6 4.6 gather_fusion.9
  1222.3 6.0 fusion
  1228.4 1044.7 %all-reduce.5.cloned.1.call-done = f32[224,1536]{0,1:T(8,128)} async-done(((f32[224,1536]{0,1:T(8,128)}), f32[224,1536]{0,1:T(8,128)}) %all-reduce.5.cloned.1.call-update) | async-done | bytes 1376272 | tf_op jit(solution)/shard_map/psum | solution.py:218
  (226 shorter events, 52.6 us)
Async XLA Ops:
  6.5 90.7 %copy-start = (f32[1536]{0:T(1024)S(1)}, f32[1536]{0:T(1024)}, u32[]{:S(2)}) copy-start(f32[1536]{0:T(1024)} %param.35) | copy-start | bytes 18436
  6.5 1139.4 %all-reduce.3.cloned.1.call-start = ((), (), s32[]{:S(2)}) async-start(), calls=%async_computation | async-start | bytes 3145728 | tf_op jit(solution)/shard_map/psum | solution.py:218
  8.3 23.3 %collective-permute-start.2 = (f32[7,32,32]{2,1,0:T(8,128)}, f32[7,32,32]{2,1,0:T(8,128)}, u32[]{:S(2)}, u32[]{:S(2)}) collective-permute-start(f32[7,32,32]{2,1,0:T(8,128)} %get-tuple-element.134), channel_id=1, source_target_pairs={{1,0},{2,1},{3,2},{4,3},{5,4},{6,5},{7,6},{8,7},{9,8},{10,9},{11,1... | collective-permute-start | bytes 86024 | tf_op jit(solution)/shard_map/ppermute | solution.py:25
  9.5 22.0 collective-permute-start.3
  16.6 15.0 collective-permute-start
  21.6 10.0 collective-permute-start.1
  36.4 22.5 collective-permute-start.4
  39.1 51.7 %copy-start.5 = (f32[1536]{0:T(1024)}, f32[1536]{0:T(1024)S(1)}, u32[]{:S(2)}) copy-start(f32[1536]{0:T(1024)S(1)} %get-tuple-element.104) | copy-start | bytes 18436
  39.1 51.7 %copy-start.7 = (f32[1536]{0:T(1024)}, f32[1536]{0:T(1024)S(1)}, u32[]{:S(2)}) copy-start(f32[1536]{0:T(1024)S(1)} %get-tuple-element.105) | copy-start | bytes 18436
  97.2 2175.9 %all-reduce.5.cloned.1.call-start = ((), (), s32[]{:S(2)}) async-start(), calls=%async_computation.1 | async-start | bytes 3145728 | tf_op jit(solution)/shard_map/psum | solution.py:218
  98.4 1051.9 %copy-start.48 = (pred[32]{0:T(512)(128)(4,1)}, pred[32]{0:T(512)(128)(4,1)S(1)}, u32[]{:S(2)}) copy-start(pred[32]{0:T(512)(128)(4,1)S(1)} %and_or_fusion) | copy-start | bytes 100
  98.5 1050.7 %copy-start.27 = (f32[128]{0:T(128)}, f32[128]{0:T(128)S(1)}, u32[]{:S(2)}) copy-start(f32[128]{0:T(128)S(1)} %get-tuple-element.111) | copy-start | bytes 1540
  98.5 1050.7 %copy-start.50 = (s32[1024]{0:T(1024)}, s32[1024]{0:T(1024)S(1)}, u32[]{:S(2)}) copy-start(s32[1024]{0:T(1024)S(1)} %pad_clamp_fusion.4) | copy-start | bytes 12292
  98.5 1050.6 %copy-start.53 = (pred[128]{0:T(512)(128)(4,1)}, pred[128]{0:T(512)(128)(4,1)S(1)}, u32[]{:S(2)}) copy-start(pred[128]{0:T(512)(128)(4,1)S(1)} %compare_and_fusion.4) | copy-start | bytes 388
  98.6 1050.6 %copy-start.29 = (f32[128]{0:T(128)}, f32[128]{0:T(128)S(1)}, u32[]{:S(2)}) copy-start(f32[128]{0:T(128)S(1)} %fusion.44) | copy-start | bytes 1540
  1152.2 12.6 collective-permute-start.8
  1153.5 10.5 collective-permute-start.7
  1154.8 9.2 collective-permute-start.5
  1161.7 3.1 collective-permute-start.6
  1168.3 23.0 %collective-permute-start.9 = (f32[7,32,1024]{2,1,0:T(8,128)S(1)}, f32[7,32,1024]{2,1,0:T(8,128)S(1)}, u32[]{:S(2)}, u32[]{:S(2)}) collective-permute-start(f32[7,32,1024]{2,1,0:T(8,128)S(1)} %multiply_add_fusion), channel_id=1, source_target_pairs={{0,128},{128,0},{1,129},{129,1},{2,130},{130,2},{3,131},{131,3},{4... | collective-permute-start | bytes 2752520 | tf_op jit(solution)/shard_map/ppermute | solution.py:33
  1228.3 1047.0 %copy-start.54 = (pred[128]{0:T(512)(128)(4,1)S(1)}, pred[128]{0:T(512)(128)(4,1)}, u32[]{:S(2)}) copy-start(pred[128]{0:T(512)(128)(4,1)} %copy-done.53) | copy-start | bytes 388
  1228.3 1047.1 %copy-start.28 = (f32[128]{0:T(128)S(1)}, f32[128]{0:T(128)}, u32[]{:S(2)}) copy-start(f32[128]{0:T(128)} %copy-done.27) | copy-start | bytes 1540
  1228.3 1047.2 %copy-start.30 = (f32[128]{0:T(128)S(1)}, f32[128]{0:T(128)}, u32[]{:S(2)}) copy-start(f32[128]{0:T(128)} %copy-done.29) | copy-start | bytes 1540
  1228.4 1053.6 %copy-start.49 = (pred[32]{0:T(512)(128)(4,1)S(1)}, pred[32]{0:T(512)(128)(4,1)}, u32[]{:S(2)}) copy-start(pred[32]{0:T(512)(128)(4,1)} %copy-done.48) | copy-start | bytes 100
  (43 other events, 414.5 us)
Sparse Core Ops, SparseCore 0:
  97.3 1048.6 all-reduce.2
  1228.5 1044.5 all-reduce.4
where the time goes:
time: 2300 us; the launch traced here: 2290 us
  waiting for transfers between devices  2130 us (93%)
  local copies, waits for them, and re-layouts  87.9 us (4%)
  starting transfers between devices  30.1 us (1%)
  other arithmetic  28.4 us (1%)
    psum x2, waiting for transfers between devices, overset(): summed_all = lax.psum(border_terms_of(source), ('colat', 'lon'))  2090 us
  transfers between devices with their start and end apart: 12, of which 5 were waited for; matrix products, arithmetic and copies ran while one was open for 0% of the time, Pallas kernels for 0%

commit v1 on v0

--- a/solution.py
+++ b/solution.py
@@ -1,7 +1,426 @@
+import functools
+
 import jax
 import jax.numpy as jnp
 from jax import lax
+from jax.experimental import pallas as pl
+from jax.experimental.pallas import tpu as pltpu
 from jax.sharding import PartitionSpec as P
+
+MESH = pl.DeviceIdType.MESH
+F32, BF16, I32 = jnp.float32, jnp.bfloat16, jnp.int32
+ROWS, COLS, WIDTH, LANES = 32, 32, 1024, 128
+POINTS, HUBS, SLOTS, SEGMENTS = 1536, 16, 4, 48
+DIFFUSE = (0.3, 0.3, 0.3, 0.4, 0.5, 0.5, 0.5)
+
+
+def iota(shape, dim):
+    return lax.broadcasted_iota(I32, shape, dim)
+
+
+def flag01(cond):
+    return jnp.where(cond, 1.0, 0.0).astype(BF16)
+
+
+def split2(x):
+    hi = x.astype(BF16)
+    return hi, (x - hi.astype(F32)).astype(BF16)
+
+
+def split3(x):
+    hi, rest = x.astype(BF16), None
+    rest = x - hi.astype(F32)
+    mid = rest.astype(BF16)
+    return hi, mid, (rest - mid.astype(F32)).astype(BF16)
+
+
+def dot(a, b):
+    return lax.dot_general(a, b, (((1,), (0,)), ((), ())), preferred_element_type=F32)
+
+
+def dot_t(a, b):
+    return lax.dot_general(a, b, (((1,), (1,)), ((), ())), preferred_element_type=F32)
+
+
+def step_kernel(
+    state, spin, device, drow, dcol, weights, angle, out, worst,
+    ext, rowsend, rowrecv, colsend, colrecv, p1send, p1recv, p2send, p2recv, summed, spread, spinx,
+    lhs_ref, pick_ref, halo_ss, halo_rs, p1_ss, p1_rs, p2_ss, p2_rs, ready,
+):
+    panel, colat, lon = (lax.axis_index(a) for a in ("panel", "colat", "lon"))
+    plane, y_lo = lon // 2, lon % 2
+    hub = colat * 2 + y_lo
+    other = 1 - panel
+
+    barrier = pltpu.get_barrier_semaphore()
+
+    def greet(**where):
+        pl.semaphore_signal(barrier, inc=1, device_id=where, device_id_type=MESH)
+
+    def peer(h):
+        return dict(colat=h // 2, lon=plane * 2 + h % 2)
+
+    @pl.loop(1, 32)
+    def _(f):
+        t = (panel * 16 + hub + f) % 32
+        h = t % 16
+        greet(panel=t // 16, colat=h // 2, lon=plane * 2 + h % 2)
+
+    @pl.loop(1, 8)
+    def _(f):
+        greet(lon=((plane + f) % 8) * 2 + y_lo)
+
+    north, south = (colat + 7) % 8, (colat + 1) % 8
+    west, east = (lon + 15) % 16, (lon + 1) % 16
+    greet(lon=west)
+    greet(lon=east)
+
+    lane = iota((1, LANES), 1)
+    group = lane // 32
+    shell = lane % 32
+
+    def pack_halo(ref, base, rnd):
+        for side, row in ((0, 0), (1, ROWS - 1)):
+            for f in range(7):
+                rowsend[rnd, side, f : f + 1, :] = ref[f, row : row + 1, base : base + WIDTH]
+            rowsend[rnd, side, 7:8, :] = jnp.zeros((1, WIDTH), F32)
+        for side, tile, have in ((0, base, 0), (1, base + WIDTH - LANES, 3)):
+            for half, fields in ((0, range(4)), (1, range(4, 7))):
+                total = jnp.zeros((ROWS, LANES), F32)
+                for f in fields:
+                    moved = pltpu.roll(ref[f, :, tile : tile + LANES], 32 * ((f % 4 - have) % 4), 1)
+                    total = jnp.where(group == f % 4, moved, total)
+                colsend[rnd, side, half] = total
+
+    def halo_copies(rnd):
+        def copy(src, dst, i, **where):
+            return pltpu.make_async_remote_copy(
+                src_ref=src, dst_ref=dst, send_sem=halo_ss.at[rnd, i], recv_sem=halo_rs.at[rnd, i],
+                device_id=where, device_id_type=MESH,
+            )
+
+        return [
+            copy(rowsend.at[rnd, 0], rowrecv.at[rnd, 1], 0, colat=north),
+            copy(rowsend.at[rnd, 1], rowrecv.at[rnd, 0], 1, colat=south),
+            copy(colsend.at[rnd, 0], colrecv.at[rnd, 1], 2, lon=west),
+            copy(colsend.at[rnd, 1], colrecv.at[rnd, 0], 3, lon=east),
+        ]
+
+    pack_halo(state, 0, 0)
+    pl.semaphore_wait(barrier, 31 + 7 + 2)
+    halos0 = halo_copies(0)
+    for copy in halos0:
+        copy.start()
+
+    @pl.loop(1, 8)
+    def _(f):
+        pl.semaphore_signal(
+            ready, inc=1, device_id=dict(lon=((plane + f) % 8) * 2 + y_lo), device_id_type=MESH
+        )
+
+    grow = (device[0:1, :] // 16) * ROWS + drow[0:1, :]
+    gcol = (device[0:1, :] % 16) * COLS + dcol[0:1, :]
+    along_row = weights[1:2, :] + weights[3:4, :]
+    along_row0 = weights[0:1, :] + weights[2:3, :]
+    along_col = weights[2:3, :] + weights[3:4, :]
+    along_col0 = weights[0:1, :] + weights[1:2, :]
+
+    def held(rr, cc):
+        return (rr >= -1) & (rr < ROWS) & (cc >= -1) & (cc < COLS)
+
+    rr, cc = grow - colat * ROWS, gcol - lon * COLS
+    mine_row = jnp.where(held(rr, cc), 1.0, 0.0)
+    mine = jnp.concatenate([mine_row[:, t * LANES : (t + 1) * LANES] for t in range(12)], axis=0)
+    mine = jnp.concatenate([mine, jnp.zeros((4, LANES), F32)], axis=0).astype(BF16)
+    up, down = iota((LANES, LANES), 0), iota((LANES, LANES), 1)
+    same = up % HUBS == down % HUBS
+    before = dot(mine, flag01(same & (up < down)))
+    whole = dot(mine, flag01(same)).astype(BF16)
+    earlier = dot(flag01(iota((16, 16), 0) > iota((16, 16), 1)), whole)
+    rank = before + earlier
+    rank_row = jnp.concatenate([rank[t : t + 1, :] for t in range(12)], axis=1)
+    point = iota((1, POINTS), 1)
+    slot = jnp.where(
+        (mine_row > 0.0) & (rank_row < SLOTS),
+        (point % HUBS) * SLOTS + rank_row.astype(I32),
+        -1,
+    )
+    slot_row = iota((LANES, 1), 0)
+    chosen = flag01(slot == (slot_row // 8) * SLOTS + slot_row % SLOTS)
+    cell = iota((ROWS, 1), 0)
+    row_w = jnp.where(cell == rr, along_row0, 0.0) + jnp.where(cell == rr + 1, along_row, 0.0)
+    col_w = jnp.where(cell == cc, along_col0, 0.0) + jnp.where(cell == cc + 1, along_col, 0.0)
+    row_hi, row_lo = split2(row_w)
+    col_hi, col_lo = split2(col_w)
+    lhs_ref[...] = dot_t(chosen, jnp.concatenate([row_hi, row_lo, row_hi, row_hi * 0], axis=0)).astype(BF16)
+    cols = dot_t(chosen, jnp.concatenate([col_hi, col_lo, col_lo * 0, col_lo * 0], axis=0)).astype(BF16)
+    cell4 = iota((LANES, WIDTH), 0)
+    expand = flag01((cell4 % 32 == iota((LANES, WIDTH), 1) // 32))
+    spread[...] = dot(cols, expand)
+    spin_parts = jnp.concatenate(list(split3(spin[0])) + [jnp.zeros((ROWS, COLS), BF16)], axis=1)
+    spinx[...] = dot(spin_parts, expand)
+
+    out_row = iota((192, 1), 0)
+    my_lane = ((out_row // 2) % 8) * HUBS + hub
+
+    def column(values):
+        tall = jnp.concatenate(
+            [jnp.broadcast_to(values[:, t * LANES : (t + 1) * LANES], (16, LANES)) for t in range(12)], axis=0
+        )
+        return jnp.sum(jnp.where(lane == my_lane, tall, 0), axis=1, keepdims=True)
+
+    source = lane // 8
+    s_rr = column(grow) - (source // 2) * ROWS
+    s_cc = column(gcol) - (plane * 2 + source % 2) * COLS
+    has = held(s_rr, s_cc)
+    count_row, count_col = iota((192, 192), 0), iota((192, 192), 1)
+    seen = dot(flag01((count_col // 2 < count_row // 2) & (count_col % 2 == 0)), flag01(has))
+    take = has & (seen.astype(I32) == lane % SLOTS) & (out_row % 2 == (lane % 8) // SLOTS)
+    pick_ref[...] = flag01(take)
+
+    every = iota((LANES, 1), 0)
+    counts = dot_t(
+        flag01(held(grow - (every // 16) * ROWS, gcol - (every % 16) * COLS)),
+        flag01(iota((LANES, 1), 0) == point % HUBS),
+    )
+    worst[...] = jnp.broadcast_to(jnp.max(counts), (8, LANES))
+
+    row_id = iota((ROWS, 1), 0)
+    inv_radius = 1.0 / (1.0 + 0.25 * (shell.astype(F32) + 0.5) / 32)
+    theta = jnp.pi / 4 + ((colat * ROWS + row_id).astype(F32) + 0.5) * (jnp.pi / 512.0)
+    metric_p = inv_radius / jnp.sin(theta)
+
+    def rate(rnd, base_ref, base_off, dst, dst_off, dt):
+        mt, mp = inv_radius, metric_p
+        mt2, mp2 = mt * mt, mp * mp
+        centre = 2.0 * (mt2 + mp2 + 1.0)
+        half_t, half_p = (0.5 * dt) * mt, (0.5 * dt) * mp
+
+        @pl.loop(0, 8)
+        def _(t):
+            off = pl.multiple_of(t * LANES, LANES)
+
+            def tile(f, k):
+                return ext[rnd, f, :, pl.ds(pl.multiple_of(off + k * LANES, LANES), LANES)]
+
+            ut, up_, ur, temp, bt, bp, br = (tile(f, 1) for f in range(7))
+            fields = (ut, up_, ur, temp, bt, bp, br)
+            at, ap, ar = ut * half_t, up_ * half_p, ur * (0.5 * dt)
+            st, sp, sr = bt * half_t, bp * half_p, br * (0.5 * dt)
+            spin_dt = spinx[:, pl.ds(off, LANES)] * dt
+            base, stretch = [], []
+            for f, c in enumerate(fields):
+                up_row = rowrecv[rnd, 0, f : f + 1, pl.ds(off, LANES)] * jnp.where(colat > 0, 1.0, 0.0)
+                down_row = rowrecv[rnd, 1, f : f + 1, pl.ds(off, LANES)] * jnp.where(colat < 7, 1.0, 0.0)
+                n = jnp.where(row_id == 0, up_row, pltpu.roll(c, 1, 0))
+                s = jnp.where(row_id == ROWS - 1, down_row, pltpu.roll(c, ROWS - 1, 0))
+                w = pltpu.roll(jnp.where(group == 3, tile(f, 0), c), 32, 1)
+                e = pltpu.roll(jnp.where(group == 0, tile(f, 2), c), 96, 1)
+                u = jnp.where(shell == 31, c, pltpu.roll(c, 127, 1))
+                d = jnp.where(shell == 0, c, pltpu.roll(c, 1, 1))
+                laplace = mt2 * (s + n) + mp2 * (e + w) + (u + d) - centre * c
+                sn, ew, ud = s - n, e - w, u - d
+                base.append((DIFFUSE[f] * dt) * laplace - (at * sn + ap * ew + ar * ud))
+                stretch.append(st * sn + sp * ew + sr * ud if f != 3 else None)
+            add = [
+                stretch[4] + spin_dt * up_,
+                stretch[5] - spin_dt * ut,
+                stretch[6] + dt * temp,
+                None,
+                stretch[0],
+                stretch[1],
+                stretch[2],
+            ]
+            for f in range(7):
+                value = base_ref[f, :, pl.ds(pl.multiple_of(base_off + off, LANES), LANES)] + base[f]
+                if add[f] is not None:
+                    value = value + add[f]
+                dst[f, :, pl.ds(pl.multiple_of(dst_off + off, LANES), LANES)] = value
+
+    def unpack_halo(rnd):
+        for side, tile, goal in ((0, 0, 3), (1, LANES + WIDTH, 0)):
+            for f in range(7):
+                have = colrecv[rnd, side, f // 4]
+                inside = (lon > 0) if side == 0 else (lon < 15)
+                ext[rnd, f, :, tile : tile + LANES] = pltpu.roll(
+                    have, 32 * ((goal - f % 4) % 4), 1
+                ) * jnp.where(inside, 1.0, 0.0)
+
+    def send_points(ref, base, rnd):
+        total = jnp.zeros((LANES, LANES), F32)
+        lhs = lhs_ref[...][:, :96]
+        row_half = (slot_row % 8) // SLOTS
+        for f in range(7):
+            hi, lo = split2(ref[f, :, base : base + WIDTH])
+            rows = dot(lhs, jnp.concatenate([hi, hi, lo], axis=0))
+            folded = jnp.zeros((LANES, LANES), F32)
+            for t in range(8):
+                folded += rows[:, t * LANES : (t + 1) * LANES] * spread[:, t * LANES : (t + 1) * LANES]
+            folded += pltpu.roll(folded, 32, 1)
+            folded += pltpu.roll(folded, 64, 1)
+            total = jnp.where((group == f % 4) & (row_half == f // 4), folded, total)
+        p1send[rnd] = total.reshape(HUBS, 8, LANES)
+        p1recv[rnd, hub] = p1send[rnd, hub]
+
+        @pl.loop(1, HUBS)
+        def _(f):
+            h = (hub + f) % HUBS
+            pltpu.make_async_remote_copy(
+                src_ref=p1send.at[rnd, h], dst_ref=p1recv.at[rnd, hub],
+                send_sem=p1_ss.at[rnd], recv_sem=p1_rs.at[rnd],
+                device_id=peer(h), device_id_type=MESH,
+            ).start()
+
+    def wait_bytes(ref, sem):
+        pltpu.make_async_copy(ref, ref, sem).wait()
+
+    def relay(rnd):
+        wait_bytes(p1recv.at[rnd, pl.ds(0, HUBS - 1)], p1_rs.at[rnd])
+        parts = jnp.concatenate(split3(p1recv[rnd].reshape(LANES, LANES)), axis=0)
+        pick = pick_ref[...]
+        picked = dot(jnp.concatenate([pick, pick, pick], axis=1), parts)
+        for s in range(SEGMENTS):
+            p2send[rnd, s] = picked[4 * s : 4 * s + 4, :]
+        if rnd == 0:
+            pl.semaphore_wait(ready, 7)
+
+        def send(s, kind, to_colat, to_lon):
+            pltpu.make_async_remote_copy(
+                src_ref=p2send.at[rnd, s], dst_ref=p2recv.at[rnd, kind, plane * HUBS + hub],
+                send_sem=p2_ss.at[rnd], recv_sem=p2_rs.at[rnd, kind],
+                device_id=dict(panel=other, colat=to_colat, lon=to_lon), device_id_type=MESH,
+            ).start()
+
+        @pl.loop(0, 16)
+        def _(i):
+            send(i, 0, 0, i)
+            send(16 + i, 1, 7, i)
+
+        @pl.loop(0, 8)
+        def _(i):
+            send(32 + i, 2, i, 0)
+            send(40 + i, 3, i, 15)
+
+    edges = [
+        (colat == 0, lon),
+        (colat == 7, 16 + lon),
+        (lon == 0, 32 + colat),
+        (lon == 15, 40 + colat),
+    ]
+
+    def place(rnd, ref, base):
+        line = iota((64, 1), 0)
+        line_point = 16 * ((line // 2) % 2) + line // 4
+        from_row = iota((64, 64), 0)
+        from_col = iota((64, 64), 1)
+        for kind, (here, segment) in enumerate(edges):
+
+            @pl.when(here)
+            def _():
+                wait_bytes(p2recv.at[rnd, kind], p2_rs.at[rnd, kind])
+                total = p2recv[rnd, kind, 0:HUBS]
+                for z in range(1, 8):
+                    total = total + p2recv[rnd, kind, z * HUBS : (z + 1) * HUBS]
+                for h in range(HUBS):
+                    summed[4 * h : 4 * h + 4, :] = total[h]
+                x = summed[...]
+                own = angle[:, pl.ds(pl.multiple_of((segment // 4) * LANES, LANES), LANES)]
+                own = jnp.where(lane == (segment % 4) * 32 + line_point, own, 0.0)
+                own = jnp.sum(own, axis=1, keepdims=True)
+                cosine, sine = jnp.cos(own), jnp.sin(own)
+                cosine = jnp.where(group < 2, cosine, 1.0)
+                swap = jnp.where(group == 0, -pltpu.roll(x, 96, 1), pltpu.roll(x, 32, 1))
+                x = cosine * x + jnp.where(group < 2, sine, 0.0) * swap
+                part = from_row // 32
+                at = from_row % 32
+                j = at if kind >= 2 else 4 * (at % 8) + at // 8
+                perm = flag01(from_col == 4 * (j % 16) + 2 * (j // 16) + part)
+                x = dot(jnp.concatenate([perm, perm, perm], axis=1), jnp.concatenate(split3(x), axis=0))
+                for f in range(7):
+                    block = x[32 * (f // 4) : 32 * (f // 4) + 32]
+                    if kind < 2:
+                        row = 0 if kind == 0 else ROWS - 1
+                        tiles = jnp.zeros((8, LANES), F32)
+                        for g in range(4):
+                            moved = pltpu.roll(block[8 * g : 8 * g + 8], 32 * ((g - f % 4) % 4), 1)
+                            tiles = jnp.where(group == g, moved, tiles)
+                        for t in range(8):
+                            ref[f, row : row + 1, base + t * LANES : base + (t + 1) * LANES] = tiles[t : t + 1]
+                    else:
+                        goal, off = (0, base) if kind == 2 else (3, base + WIDTH - LANES)
+                        moved = pltpu.roll(block, 32 * ((goal - f % 4) % 4), 1)
+                        now = ref[f, :, off : off + LANES]
+                        corner = ((row_id == 0) & (colat == 0)) | ((row_id == ROWS - 1) & (colat == 7))
+                        blend = jnp.where(corner, 0.5 * (moved + now), moved)
+                        ref[f, :, off : off + LANES] = jnp.where(group == goal, blend, now)
+
+    for f in range(7):
+        ext[0, f, :, LANES : LANES + WIDTH] = state[f]
+    for copy in halos0:
+        copy.wait_recv()
+    unpack_halo(0)
+    rate(0, state, 0, ext.at[1], LANES, 0.1)
+    send_points(ext.at[1], LANES, 0)
+    pack_halo(ext.at[1], LANES, 1)
+    halos1 = halo_copies(1)
+    for copy in halos1:
+        copy.start()
+    relay(0)
+    for copy in halos1:
+        copy.wait_recv()
+    unpack_halo(1)
+    place(0, ext.at[1], LANES)
+    rate(1, state, 0, out, 0, 0.2)
+    send_points(out, 0, 1)
+    relay(1)
+    place(1, out, 0)
+    for copy in halos0 + halos1:
+        copy.wait_send()
+    for rnd in range(2):
+        wait_bytes(p1send.at[rnd, pl.ds(0, HUBS - 1)], p1_ss.at[rnd])
+        wait_bytes(p2send.at[rnd], p2_ss.at[rnd])
+
+
+def fast_step(state, spin, device, drow, dcol, weights, angle):
+    vmem = pl.BlockSpec(memory_space=pltpu.VMEM)
+    scratch = lambda *shape: pltpu.VMEM(shape, F32)
+    return pl.pallas_call(
+        step_kernel,
+        out_shape=(
+            jax.ShapeDtypeStruct((7, ROWS, WIDTH), F32),
+            jax.ShapeDtypeStruct((8, LANES), F32),
+        ),
+        in_specs=[vmem] * 7,
+        out_specs=(vmem, vmem),
+        scratch_shapes=[
+            scratch(2, 7, ROWS, WIDTH + 2 * LANES),
+            scratch(2, 2, 8, WIDTH),
+            scratch(2, 2, 8, WIDTH),
+            scratch(2, 2, 2, ROWS, LANES),
+            scratch(2, 2, 2, ROWS, LANES),
+            scratch(2, HUBS, 8, LANES),
+            scratch(2, HUBS, 8, LANES),
+            scratch(2, SEGMENTS, 4, LANES),
+            scratch(2, 4, 8 * HUBS, 4, LANES),
+            scratch(64, LANES),
+            scratch(LANES, WIDTH),
+            scratch(ROWS, WIDTH),
+            pltpu.VMEM((LANES, LANES), BF16),
+            pltpu.VMEM((192, LANES), BF16),
+            pltpu.SemaphoreType.DMA((2, 4)),
+            pltpu.SemaphoreType.DMA((2, 4)),
+            pltpu.SemaphoreType.DMA((2,)),
+            pltpu.SemaphoreType.DMA((2,)),
+            pltpu.SemaphoreType.DMA((2,)),
+            pltpu.SemaphoreType.DMA((2, 4)),
+            pltpu.SemaphoreType.REGULAR,
+        ],
+        compiler_params=pltpu.CompilerParams(
+            collective_id=0, has_side_effects=True, vmem_limit_bytes=48 * 2**20
+        ),
+        name="dynamo_step",
+    )(state, spin, device, drow, dcol, weights, angle)
+
 
 FIELDS = 7
 NR = 32
@@ -100,7 +519,7 @@
     return index_map
 
 
-def on_device(state, spin, donor_device, donor_row, donor_col, corner_weights, border_angle):
+def general_step(state, spin, donor_device, donor_row, donor_col, corner_weights, border_angle):
     fields = state[0]
     lat_rows = fields.shape[1]
     width = fields.shape[2]
@@ -227,6 +646,19 @@
     return advanced[None]
 
 
+def on_device(state, spin, donor_device, donor_row, donor_col, corner_weights, border_angle):
+    fast, worst = fast_step(
+        state[0], spin, donor_device, donor_row, donor_col, corner_weights, border_angle[None]
+    )
+    return lax.cond(
+        worst[0, 0] > SLOTS,
+        lambda: general_step(
+            state, spin, donor_device, donor_row, donor_col, corner_weights, border_angle
+        ),
+        lambda: fast[None],
+    )
+
+
 def solution(mesh):
     placed = (P("panel", None, "colat", "lon"), P("panel", "colat", "lon"), P(), P(), P(), P(), P())
     return jax.shard_map(

time: 2300 us -> 68.7 us (0.03)
  waiting for transfers between devices: 2130 us -> 0 us
  local copies, waits for them, and re-layouts: 87.9 us -> 3.42 us
  Pallas kernels: 0 us -> 50.8 us
  starting transfers between devices: 30.1 us -> 0 us
  other arithmetic: 28.4 us -> 0 us
    psum x2 -> x0, waiting for transfers between devices: 2090 us -> none  [overset(): summed_all = lax.psum(border_terms_of(source), ('colat', 'lon'))]
    pallas_call x0 -> x1, Pallas kernels: none -> 50.8 us  [fast_step(): pl.pallas_call(step_kernel, out_shape=(jax.ShapeDtypeStruct((7, ROWS, WID...]
    gather x11 -> x0, local copies, waits for them, and re-layouts: 41.8 us -> none  [the longest x8 36.2 us: border_terms_of(): jnp.take(flat_block, cell_index[corner], axis=1) * weight[None, :]]
    ppermute x10 -> x0, waiting for transfers between devices: 41.1 us -> none  [the longest x2 40.4 us: partner(): return lax.ppermute(value, axis, pairs)]
    ppermute x10 -> x0, starting transfers between devices: 30.1 us -> none  [the longest x4 14.5 us: with_halo(): lax.ppermute(lax.slice_in_dim(block, 0, width, axis=dim), axis, backward)]
    reshape x11 -> x0, local copies, waits for them, and re-layouts: 28.1 us -> none  [the longest x4 21.3 us: border_terms_of(): flat_block = source.reshape(FIELDS, lat_rows, lon_cells, NR).transpose(0,...]
  transfers between devices with their start and end apart: 12 -> 0, of which waited for: 5 -> 0; matrix products, arithmetic and copies ran while one was open for 0% -> 0% of each run, Pallas kernels for 0% -> 0%
where the time goes in v1:
time: 68.7 us; the launch traced here: 68.5 us
  Pallas kernels  50.8 us (74%)
  between operations  14 us (20%)
  local copies, waits for them, and re-layouts  3.42 us (5%)
    pallas_call x1, Pallas kernels, fast_step(): pl.pallas_call(step_kernel, out_shape=(jax.ShapeDtypeStruct((7, ROWS, WID...  50.8 us
    unnamed x1, local copies, waits for them, and re-layouts  2.2 us

profile of v1, /device:TPU:1, one launch (start us, length us, event | category | flops | bytes accessed | tf_op | source)
XLA Modules:
  0.0 68.5 jit_solution(15128957907357184413)
XLA Ops:
  6.5 0.7 %broadcast_in_dim.118.angle = f32[1,1536]{1,0:T(1,128)S(1)} reshape(f32[1536]{0:T(1024)} %param.37) | data formatting | bytes 12288 | tf_op jit(solution)/shard_map/broadcast_in_dim | solution.py:651
  7.2 50.8 %dynamo_step.1 = (f32[7,32,1024]{2,1,0:T(8,128)}, f32[8,128]{1,0:T(8,128)S(1)}) custom-call(f32[7,32,1024]{2,1,0:T(8,128)} %bitcast.160, f32[1,32,32]{2,1,0:T(8,128)} %spin.1, s32[4,1536]{1,0:T(4,128)} %device.1, s32[4,1536]{1,0:T(4,128)} %drow.1, s32[4,1536]{1,0:T(4,128)} %dcol.1, f32[4,1536]{1,0:T(4,128)} %weights.1, f32[1,1536]{1,0:T(1,128)S(1)} %broadcast_in_dim.118.angle), custom_call_target="tpu_custom_call" | custom-call | tf_op jit(solution)/shard_map/dynamo_step/pallas_call | solution.py:387
  58.1 0.5 slice.553
  59.2 0.2 conditional.1
  59.5 2.2 %copy.224 = f32[1,7,32,1024]{3,2,1,0:T(8,128)} copy(f32[1,7,32,1024]{3,2,1,0:T(8,128)} %get-tuple-element.138) | data formatting | bytes 1835008

commit v2 on v1

--- a/solution.py
+++ b/solution.py
@@ -43,9 +43,10 @@
 
 
 def step_kernel(
+    rounds,
     state, spin, device, drow, dcol, weights, angle, out, worst,
     ext, rowsend, rowrecv, colsend, colrecv, p1send, p1recv, p2send, p2recv, summed, spread, spinx,
-    lhs_ref, pick_ref, halo_ss, halo_rs, p1_ss, p1_rs, p2_ss, p2_rs, ready,
+    lhs_ref, pick_ref, hub_sum, halo_ss, halo_rs, p1_ss, p1_rs, p2_ss, p2_rs, ready,
 ):
     panel, colat, lon = (lax.axis_index(a) for a in ("panel", "colat", "lon"))
     plane, y_lo = lon // 2, lon % 2
@@ -140,23 +141,26 @@
     rank = before + earlier
     rank_row = jnp.concatenate([rank[t : t + 1, :] for t in range(12)], axis=1)
     point = iota((1, POINTS), 1)
-    slot = jnp.where(
-        (mine_row > 0.0) & (rank_row < SLOTS),
-        (point % HUBS) * SLOTS + rank_row.astype(I32),
-        -1,
-    )
     slot_row = iota((LANES, 1), 0)
-    chosen = flag01(slot == (slot_row // 8) * SLOTS + slot_row % SLOTS)
     cell = iota((ROWS, 1), 0)
     row_w = jnp.where(cell == rr, along_row0, 0.0) + jnp.where(cell == rr + 1, along_row, 0.0)
     col_w = jnp.where(cell == cc, along_col0, 0.0) + jnp.where(cell == cc + 1, along_col, 0.0)
     row_hi, row_lo = split2(row_w)
     col_hi, col_lo = split2(col_w)
-    lhs_ref[...] = dot_t(chosen, jnp.concatenate([row_hi, row_lo, row_hi, row_hi * 0], axis=0)).astype(BF16)
-    cols = dot_t(chosen, jnp.concatenate([col_hi, col_lo, col_lo * 0, col_lo * 0], axis=0)).astype(BF16)
+    row_parts = jnp.concatenate([row_hi, row_lo, row_hi, row_hi * 0], axis=0)
+    col_parts = jnp.concatenate([col_hi, col_lo, col_lo * 0, col_lo * 0], axis=0)
     cell4 = iota((LANES, WIDTH), 0)
     expand = flag01((cell4 % 32 == iota((LANES, WIDTH), 1) // 32))
-    spread[...] = dot(cols, expand)
+
+    def fill_slots(turn):
+        order = rank_row.astype(I32) - turn * SLOTS
+        slot = jnp.where(
+            (mine_row > 0.0) & (order >= 0) & (order < SLOTS), (point % HUBS) * SLOTS + order, -1
+        )
+        chosen = flag01(slot == (slot_row // 8) * SLOTS + slot_row % SLOTS)
+        lhs_ref[...] = dot_t(chosen, row_parts).astype(BF16)
+        spread[...] = dot(dot_t(chosen, col_parts).astype(BF16), expand)
+
     spin_parts = jnp.concatenate(list(split3(spin[0])) + [jnp.zeros((ROWS, COLS), BF16)], axis=1)
     spinx[...] = dot(spin_parts, expand)
 
@@ -175,8 +179,15 @@
     has = held(s_rr, s_cc)
     count_row, count_col = iota((192, 192), 0), iota((192, 192), 1)
     seen = dot(flag01((count_col // 2 < count_row // 2) & (count_col % 2 == 0)), flag01(has))
-    take = has & (seen.astype(I32) == lane % SLOTS) & (out_row % 2 == (lane % 8) // SLOTS)
-    pick_ref[...] = flag01(take)
+
+    def fill_picks(turn):
+        slot = seen.astype(I32) - turn * SLOTS
+        take = has & (slot == lane % SLOTS) & (out_row % 2 == (lane % 8) // SLOTS)
+        pick_ref[...] = flag01(take)
+
+    if rounds == 1:
+        fill_slots(0)
+        fill_picks(0)
 
     every = iota((LANES, 1), 0)
     counts = dot_t(
@@ -247,38 +258,62 @@
                 ) * jnp.where(inside, 1.0, 0.0)
 
     def send_points(ref, base, rnd):
-        total = jnp.zeros((LANES, LANES), F32)
-        lhs = lhs_ref[...][:, :96]
         row_half = (slot_row % 8) // SLOTS
-        for f in range(7):
-            hi, lo = split2(ref[f, :, base : base + WIDTH])
-            rows = dot(lhs, jnp.concatenate([hi, hi, lo], axis=0))
-            folded = jnp.zeros((LANES, LANES), F32)
-            for t in range(8):
-                folded += rows[:, t * LANES : (t + 1) * LANES] * spread[:, t * LANES : (t + 1) * LANES]
-            folded += pltpu.roll(folded, 32, 1)
-            folded += pltpu.roll(folded, 64, 1)
-            total = jnp.where((group == f % 4) & (row_half == f // 4), folded, total)
-        p1send[rnd] = total.reshape(HUBS, 8, LANES)
-        p1recv[rnd, hub] = p1send[rnd, hub]
-
-        @pl.loop(1, HUBS)
-        def _(f):
-            h = (hub + f) % HUBS
-            pltpu.make_async_remote_copy(
-                src_ref=p1send.at[rnd, h], dst_ref=p1recv.at[rnd, hub],
-                send_sem=p1_ss.at[rnd], recv_sem=p1_rs.at[rnd],
-                device_id=peer(h), device_id_type=MESH,
-            ).start()
+
+        def turn_points(turn):
+            total = jnp.zeros((LANES, LANES), F32)
+            lhs = lhs_ref[...][:, :96]
+            for f in range(7):
+                hi, lo = split2(ref[f, :, base : base + WIDTH])
+                rows = dot(lhs, jnp.concatenate([hi, hi, lo], axis=0))
+                folded = jnp.zeros((LANES, LANES), F32)
+                for t in range(8):
+                    folded += rows[:, t * LANES : (t + 1) * LANES] * spread[:, t * LANES : (t + 1) * LANES]
+                folded += pltpu.roll(folded, 32, 1)
+                folded += pltpu.roll(folded, 64, 1)
+                total = jnp.where((group == f % 4) & (row_half == f // 4), folded, total)
+            p1send[rnd, turn] = total.reshape(HUBS, 8, LANES)
+            p1recv[rnd, turn, hub] = p1send[rnd, turn, hub]
+
+            @pl.loop(1, HUBS)
+            def _(f):
+                h = (hub + f) % HUBS
+                pltpu.make_async_remote_copy(
+                    src_ref=p1send.at[rnd, turn, h], dst_ref=p1recv.at[rnd, turn, hub],
+                    send_sem=p1_ss.at[rnd, turn], recv_sem=p1_rs.at[rnd, turn],
+                    device_id=peer(h), device_id_type=MESH,
+                ).start()
+
+        if rounds == 1:
+            turn_points(0)
+        else:
+
+            @pl.loop(0, rounds)
+            def _(turn):
+                fill_slots(turn)
+                turn_points(turn)
 
     def wait_bytes(ref, sem):
         pltpu.make_async_copy(ref, ref, sem).wait()
 
     def relay(rnd):
-        wait_bytes(p1recv.at[rnd, pl.ds(0, HUBS - 1)], p1_rs.at[rnd])
-        parts = jnp.concatenate(split3(p1recv[rnd].reshape(LANES, LANES)), axis=0)
-        pick = pick_ref[...]
-        picked = dot(jnp.concatenate([pick, pick, pick], axis=1), parts)
+        def turn_sum(turn):
+            wait_bytes(p1recv.at[rnd, turn, pl.ds(0, HUBS - 1)], p1_rs.at[rnd, turn])
+            parts = jnp.concatenate(split3(p1recv[rnd, turn].reshape(LANES, LANES)), axis=0)
+            pick = pick_ref[...]
+            return dot(jnp.concatenate([pick, pick, pick], axis=1), parts)
+
+        if rounds == 1:
+            picked = turn_sum(0)
+        else:
+            hub_sum[...] = jnp.zeros_like(hub_sum)
+
+            @pl.loop(0, rounds)
+            def _(turn):
+                fill_picks(turn)
+                hub_sum[...] += turn_sum(turn)
+
+            picked = hub_sum[...]
         for s in range(SEGMENTS):
             p2send[rnd, s] = picked[4 * s : 4 * s + 4, :]
         if rnd == 0:
@@ -377,15 +412,16 @@
     for copy in halos0 + halos1:
         copy.wait_send()
     for rnd in range(2):
-        wait_bytes(p1send.at[rnd, pl.ds(0, HUBS - 1)], p1_ss.at[rnd])
+        for turn in range(rounds):
+            wait_bytes(p1send.at[rnd, turn, pl.ds(0, HUBS - 1)], p1_ss.at[rnd, turn])
         wait_bytes(p2send.at[rnd], p2_ss.at[rnd])
 
 
-def fast_step(state, spin, device, drow, dcol, weights, angle):
+def step(rounds, state, spin, device, drow, dcol, weights, angle):
     vmem = pl.BlockSpec(memory_space=pltpu.VMEM)
     scratch = lambda *shape: pltpu.VMEM(shape, F32)
     return pl.pallas_call(
-        step_kernel,
+        functools.partial(step_kernel, rounds),
         out_shape=(
             jax.ShapeDtypeStruct((7, ROWS, WIDTH), F32),
             jax.ShapeDtypeStruct((8, LANES), F32),
@@ -398,8 +434,8 @@
             scratch(2, 2, 8, WIDTH),
             scratch(2, 2, 2, ROWS, LANES),
             scratch(2, 2, 2, ROWS, LANES),
-            scratch(2, HUBS, 8, LANES),
-            scratch(2, HUBS, 8, LANES),
+            scratch(2, rounds, HUBS, 8, LANES),
+            scratch(2, rounds, HUBS, 8, LANES),
             scratch(2, SEGMENTS, 4, LANES),
             scratch(2, 4, 8 * HUBS, 4, LANES),
             scratch(64, LANES),
@@ -407,256 +443,28 @@
             scratch(ROWS, WIDTH),
             pltpu.VMEM((LANES, LANES), BF16),
             pltpu.VMEM((192, LANES), BF16),
+            scratch(192, LANES),
             pltpu.SemaphoreType.DMA((2, 4)),
             pltpu.SemaphoreType.DMA((2, 4)),
-            pltpu.SemaphoreType.DMA((2,)),
-            pltpu.SemaphoreType.DMA((2,)),
+            pltpu.SemaphoreType.DMA((2, rounds)),
+            pltpu.SemaphoreType.DMA((2, rounds)),
             pltpu.SemaphoreType.DMA((2,)),
             pltpu.SemaphoreType.DMA((2, 4)),
             pltpu.SemaphoreType.REGULAR,
         ],
         compiler_params=pltpu.CompilerParams(
-            collective_id=0, has_side_effects=True, vmem_limit_bytes=48 * 2**20
+            collective_id=0 if rounds == 1 else 1, has_side_effects=True, vmem_limit_bytes=48 * 2**20
         ),
-        name="dynamo_step",
+        name="dynamo_step" if rounds == 1 else "general_step",
     )(state, spin, device, drow, dcol, weights, angle)
 
 
-FIELDS = 7
-NR = 32
-
-
-viscosity = 0.3
-conduction = 0.4
-resistance = 0.5
-buoyancy = 1.0
-timestep = 0.2
-
-
-def with_halo(block, sides, width):
-    for axis, dim in sides:
-        count = lax.axis_size(axis)
-        forward = [(i, i + 1) for i in range(count - 1)]
-        backward = [(target, source) for source, target in forward]
-        low = lax.ppermute(
-            lax.slice_in_dim(block, block.shape[dim] - width, None, axis=dim), axis, forward
-        )
-        high = lax.ppermute(lax.slice_in_dim(block, 0, width, axis=dim), axis, backward)
-        block = jnp.concatenate([low, block, high], axis=dim)
-    return block
-
-
-def partner(value, axis, distance):
-    mask = 2**distance
-    pairs = [(source, source ^ mask) for source in range(lax.axis_size(axis))]
-    return lax.ppermute(value, axis, pairs)
-
-
-def field_rates(
-    fields,
-    north_cells,
-    south_cells,
-    west_cells,
-    east_cells,
-    upper_cells,
-    lower_cells,
-    metric_t,
-    metric_p,
-    spin_cells,
-):
-    colat_slope = metric_t * (0.5 * (south_cells - north_cells))
-    lon_slope = metric_p * (0.5 * (east_cells - west_cells))
-    radial_slope = 0.5 * (upper_cells - lower_cells)
-    laplace = (
-        metric_t * metric_t * (south_cells + north_cells - 2.0 * fields)
-        + metric_p * metric_p * (east_cells + west_cells - 2.0 * fields)
-        + (upper_cells + lower_cells - 2.0 * fields)
-    )
-    advected = fields[0] * colat_slope + fields[1] * lon_slope + fields[2] * radial_slope
-    stretched = fields[4] * colat_slope + fields[5] * lon_slope + fields[6] * radial_slope
-    diffuse_rate = jnp.array(
-        [viscosity, viscosity, viscosity, conduction, resistance, resistance, resistance],
-        jnp.float32,
-    )
-    diffuse_rate = diffuse_rate.reshape((7,) + (1,) * (fields.ndim - 1))
-    base_rate = diffuse_rate * laplace - advected
-    return jnp.stack(
-        [
-            base_rate[0] + stretched[4] + spin_cells * fields[1],
-            base_rate[1] + stretched[5] - spin_cells * fields[0],
-            base_rate[2] + stretched[6] + buoyancy * fields[3],
-            base_rate[3],
-            base_rate[4] + stretched[0],
-            base_rate[5] + stretched[1],
-            base_rate[6] + stretched[2],
-        ]
-    )
-
-
-def slot_map(colat_block, lon_block, lat_rows, lon_cells, n_colat, n_lon):
-    slot_count = 2 * (lat_rows + lon_cells)
-    lat_total = lat_rows * n_colat
-    lon_total = lon_cells * n_lon
-    slot_ids = jnp.arange(slot_count, dtype=jnp.int32)[None, :]
-    colat_block = colat_block[:, None]
-    lon_block = lon_block[:, None]
-    is_top = slot_ids < lon_cells
-    is_bottom = (slot_ids >= lon_cells) & (slot_ids < 2 * lon_cells)
-    is_left = (slot_ids >= 2 * lon_cells) & (slot_ids < 2 * lon_cells + lat_rows)
-    along_lon = lon_block * lon_cells + slot_ids
-    along_lat = colat_block * lat_rows + slot_ids - 2 * lon_cells
-    index_map = jnp.where(
-        is_top,
-        along_lon,
-        jnp.where(
-            is_bottom,
-            lon_total + along_lon - lon_cells,
-            jnp.where(
-                is_left, 2 * lon_total + along_lat, 2 * lon_total + lat_total + along_lat - lat_rows
-            ),
-        ),
-    )
-    return index_map
-
-
-def general_step(state, spin, donor_device, donor_row, donor_col, corner_weights, border_angle):
-    fields = state[0]
-    lat_rows = fields.shape[1]
-    width = fields.shape[2]
-    lon_cells = width // NR
-    n_colat = lax.axis_size("colat")
-    n_lon = lax.axis_size("lon")
-    colat_block = lax.axis_index("colat")
-    lon_block = lax.axis_index("lon")
-    shell_index = jnp.arange(width, dtype=jnp.int32) % NR
-    shell_float = shell_index.astype(jnp.float32)
-    inv_radius = 1.0 / (1.0 + 0.25 * (shell_float + 0.5) / NR)
-    row_number = (colat_block * lat_rows + jnp.arange(lat_rows, dtype=jnp.int32)).astype(
-        jnp.float32
-    )
-    colat_angle = jnp.pi / 4 + (row_number + 0.5) * (jnp.pi / (2.0 * (lat_rows * n_colat)))
-    metric_p = inv_radius[None, :] / jnp.sin(colat_angle)[:, None]
-    spin_cells = jnp.repeat(spin[0], NR, axis=1)
-    own_slots = slot_map(
-        jnp.reshape(colat_block, (1,)),
-        jnp.reshape(lon_block, (1,)),
-        lat_rows,
-        lon_cells,
-        n_colat,
-        n_lon,
-    )[0]
-    slot_angle = jnp.take(border_angle, own_slots)
-    cosine = jnp.cos(slot_angle)
-    sine_part = jnp.sin(slot_angle)
-    cell_index = donor_row * lon_cells + donor_col
-    is_mine = donor_device == colat_block * n_lon + lon_block
-    per_device = FIELDS * NR
-
-    def tendency(current):
-        colat_ext = with_halo(current, (("colat", 1),), 1)
-        lon_ext = with_halo(current, (("lon", 2),), NR)
-        north_cells = colat_ext[:, :-2]
-        south_cells = colat_ext[:, 2:]
-        west_cells = lon_ext[:, :, : -2 * NR]
-        east_cells = lon_ext[:, :, 2 * NR :]
-        upper_cells = jnp.where(
-            shell_index == NR - 1,
-            current,
-            jnp.concatenate([current[..., 1:], current[..., -1:]], axis=-1),
-        )
-        lower_cells = jnp.where(
-            shell_index == 0,
-            current,
-            jnp.concatenate([current[..., :1], current[..., :-1]], axis=-1),
-        )
-        return field_rates(
-            current,
-            north_cells,
-            south_cells,
-            west_cells,
-            east_cells,
-            upper_cells,
-            lower_cells,
-            inv_radius,
-            metric_p,
-            spin_cells,
-        )
-
-    def border_terms_of(source):
-        flat_block = (
-            source.reshape(FIELDS, lat_rows, lon_cells, NR)
-            .transpose(0, 3, 1, 2)
-            .reshape(per_device, lat_rows * lon_cells)
-        )
-        summed = jnp.zeros((per_device, donor_row.shape[1]), jnp.float32)
-        for corner in range(4):
-            weight = jnp.where(is_mine[corner], corner_weights[corner], 0.0)
-            summed = summed + jnp.take(flat_block, cell_index[corner], axis=1) * weight[None, :]
-        return summed
-
-    def rotate(picked):
-        return jnp.stack(
-            [
-                cosine * picked[0] - sine_part * picked[1],
-                sine_part * picked[0] + cosine * picked[1],
-                picked[2],
-                picked[3],
-                cosine * picked[4] - sine_part * picked[5],
-                sine_part * picked[4] + cosine * picked[5],
-                picked[6],
-            ]
-        )
-
-    def place_border(target, turned):
-        top_row = turned[:, :, 0:lon_cells].transpose(0, 2, 1).reshape(FIELDS, width)
-        bottom_row = (
-            turned[:, :, lon_cells : 2 * lon_cells].transpose(0, 2, 1).reshape(FIELDS, width)
-        )
-        left_col = turned[:, :, 2 * lon_cells : 2 * lon_cells + lat_rows].transpose(0, 2, 1)
-        right_col = turned[:, :, 2 * lon_cells + lat_rows :].transpose(0, 2, 1)
-        target = target.at[:, 0, :].set(jnp.where(colat_block == 0, top_row, target[:, 0, :]))
-        target = target.at[:, lat_rows - 1, :].set(
-            jnp.where(colat_block == n_colat - 1, bottom_row, target[:, lat_rows - 1, :])
-        )
-        row_ids = jnp.arange(lat_rows)
-        edge_row = (row_ids == 0) & (colat_block == 0) | (row_ids == lat_rows - 1) & (
-            colat_block == n_colat - 1
-        )
-        current = target[:, :, 0:NR]
-        blended = jnp.where(edge_row[None, :, None], 0.5 * (left_col + current), left_col)
-        target = target.at[:, :, 0:NR].set(jnp.where(lon_block == 0, blended, current))
-        current = target[:, :, width - NR :]
-        blended = jnp.where(edge_row[None, :, None], 0.5 * (right_col + current), right_col)
-        target = target.at[:, :, width - NR :].set(
-            jnp.where(lon_block == n_lon - 1, blended, current)
-        )
-        return target
-
-    def overset(target):
-        source = partner(target, "panel", 0)
-        summed_all = lax.psum(border_terms_of(source), ("colat", "lon"))
-        picked = jnp.take(summed_all, own_slots, axis=1)
-        turned = rotate(picked.reshape(FIELDS, NR, -1))
-        return place_border(target, turned)
-
-    tendency_now = tendency(fields)
-    middle = overset(fields + 0.5 * timestep * tendency_now)
-    tendency_now = tendency(middle)
-    advanced = overset(fields + timestep * tendency_now)
+def on_device(state, spin, donor_device, donor_row, donor_col, corner_weights, border_angle):
+    args = (state[0], spin, donor_device, donor_row, donor_col, corner_weights, border_angle[None])
+    fast, worst = step(1, *args)
+    turns = POINTS // HUBS // SLOTS
+    advanced = lax.cond(worst[0, 0] > SLOTS, lambda: step(turns, *args)[0], lambda: fast)
     return advanced[None]
-
-
-def on_device(state, spin, donor_device, donor_row, donor_col, corner_weights, border_angle):
-    fast, worst = fast_step(
-        state[0], spin, donor_device, donor_row, donor_col, corner_weights, border_angle[None]
-    )
-    return lax.cond(
-        worst[0, 0] > SLOTS,
-        lambda: general_step(
-            state, spin, donor_device, donor_row, donor_col, corner_weights, border_angle
-        ),
-        lambda: fast[None],
-    )
 
 
 def solution(mesh):

time: 68.7 us -> 53.1 us (0.77)
  between operations: 14 us -> 0.74 us
  local copies, waits for them, and re-layouts: 3.42 us -> 2.25 us
  Pallas kernels: 50.8 us -> 50 us
    unnamed x1 -> x13, local copies, waits for them, and re-layouts: 2.2 us -> 0.96 us
    pallas_call x1, Pallas kernels: 50.8 us -> 50 us  [step(): pl.pallas_call(functools.partial(step_kernel, rounds), out_shape=(jax.Sha...]
where the time goes in v2:
time: 53.1 us; the launch traced here: 53 us
  Pallas kernels  50 us (94%)
  local copies, waits for them, and re-layouts  2.25 us (4%)
  between operations  0.74 us (1%)
    pallas_call x1, Pallas kernels, step(): pl.pallas_call(functools.partial(step_kernel, rounds), out_shape=(jax.Sha...  50 us

profile of v2, /device:TPU:1, one launch (start us, length us, event | category | flops | bytes accessed | tf_op | source)
XLA Modules:
  0.0 53.0 jit_solution(10250547469164173574)
XLA Ops:
  0.0 0.0 copy-start.5
  0.0 0.0 copy-start
  0.0 0.8 %broadcast_in_dim.10.angle = f32[1,1536]{1,0:T(1,128)S(1)} reshape(f32[1536]{0:T(1024)} %param.15) | data formatting | bytes 12288 | tf_op jit(solution)/shard_map/broadcast_in_dim | solution.py:463
  0.8 0.0 copy-done.5
  0.8 0.0 copy-start.1
  0.8 0.0 copy-start.2
  0.8 0.0 copy-start.3
  0.8 0.0 copy-start.4
  0.8 50.0 %dynamo_step.1 = (f32[7,32,1024]{2,1,0:T(8,128)S(1)}, f32[8,128]{1,0:T(8,128)S(1)}) custom-call(f32[7,32,1024]{2,1,0:T(8,128)} %bitcast.4, f32[1,32,32]{2,1,0:T(8,128)S(1)} %copy-done.5, s32[4,1536]{1,0:T(4,128)} %device.1, s32[4,1536]{1,0:T(4,128)} %drow.1, s32[4,1536]{1,0:T(4,128)} %dcol.1, f32[4,1536]{1,0:T(4,128)} %weights.1, ...), custom_call_target="tpu_custom_call" | custom-call | tf_op jit(solution)/shard_map/dynamo_step/pallas_call | solution.py:423
  50.8 0.5 slice.3
  52.0 0.0 copy-done
  52.0 0.0 copy-done.1
  52.0 0.0 copy-done.2
  52.0 0.0 copy-done.3
  52.0 0.0 copy-done.4
  52.1 0.9 %copy.14 = f32[1,7,32,1024]{3,2,1,0:T(8,128)} copy(f32[1,7,32,1024]{3,2,1,0:T(8,128)S(1)} %get-tuple-element.37) | data formatting | bytes 1835008
  (1 shorter events, 0.0 us)
Async XLA Ops:
  0.0 0.8 %copy-start.5 = (f32[1,32,32]{2,1,0:T(8,128)S(1)}, f32[1,32,32]{2,1,0:T(8,128)}, u32[]{:S(2)}) copy-start(f32[1,32,32]{2,1,0:T(8,128)} %spin.1) | copy-start | bytes 12292
  0.0 52.0 %copy-start = (f32[1,7,32,1024]{3,2,1,0:T(8,128)S(1)}, f32[1,7,32,1024]{3,2,1,0:T(8,128)}, u32[]{:S(2)}) copy-start(f32[1,7,32,1024]{3,2,1,0:T(8,128)} %param.9) | copy-start | bytes 2752516
  0.8 51.2 %copy-start.1 = (s32[4,1536]{1,0:T(4,128)S(1)}, s32[4,1536]{1,0:T(4,128)}, u32[]{:S(2)}) copy-start(s32[4,1536]{1,0:T(4,128)} %device.1) | copy-start | bytes 73732
  0.8 51.2 %copy-start.2 = (s32[4,1536]{1,0:T(4,128)S(1)}, s32[4,1536]{1,0:T(4,128)}, u32[]{:S(2)}) copy-start(s32[4,1536]{1,0:T(4,128)} %drow.1) | copy-start | bytes 73732
  0.8 51.2 %copy-start.3 = (s32[4,1536]{1,0:T(4,128)S(1)}, s32[4,1536]{1,0:T(4,128)}, u32[]{:S(2)}) copy-start(s32[4,1536]{1,0:T(4,128)} %dcol.1) | copy-start | bytes 73732
  0.8 51.2 %copy-start.4 = (f32[4,1536]{1,0:T(4,128)S(1)}, f32[4,1536]{1,0:T(4,128)}, u32[]{:S(2)}) copy-start(f32[4,1536]{1,0:T(4,128)} %weights.1) | copy-start | bytes 73732

commit v3 on v2

--- a/solution.py
+++ b/solution.py
@@ -10,6 +10,7 @@
 MESH = pl.DeviceIdType.MESH
 F32, BF16, I32 = jnp.float32, jnp.bfloat16, jnp.int32
 ROWS, COLS, WIDTH, LANES = 32, 32, 1024, 128
+HELD = 64
 POINTS, HUBS, SLOTS, SEGMENTS = 1536, 16, 4, 48
 DIFFUSE = (0.3, 0.3, 0.3, 0.4, 0.5, 0.5, 0.5)
 
@@ -44,7 +45,7 @@
 
 def step_kernel(
     rounds,
-    state, spin, device, drow, dcol, weights, angle, out, worst,
+    state, spin, device, drow, dcol, weights, angle, out, overfull,
     ext, rowsend, rowrecv, colsend, colrecv, p1send, p1recv, p2send, p2recv, summed, spread, spinx,
     lhs_ref, pick_ref, hub_sum, halo_ss, halo_rs, p1_ss, p1_rs, p2_ss, p2_rs, ready,
 ):
@@ -107,18 +108,6 @@
             copy(colsend.at[rnd, 1], colrecv.at[rnd, 0], 3, lon=east),
         ]
 
-    pack_halo(state, 0, 0)
-    pl.semaphore_wait(barrier, 31 + 7 + 2)
-    halos0 = halo_copies(0)
-    for copy in halos0:
-        copy.start()
-
-    @pl.loop(1, 8)
-    def _(f):
-        pl.semaphore_signal(
-            ready, inc=1, device_id=dict(lon=((plane + f) % 8) * 2 + y_lo), device_id_type=MESH
-        )
-
     grow = (device[0:1, :] // 16) * ROWS + drow[0:1, :]
     gcol = (device[0:1, :] % 16) * COLS + dcol[0:1, :]
     along_row = weights[1:2, :] + weights[3:4, :]
@@ -141,7 +130,7 @@
     rank = before + earlier
     rank_row = jnp.concatenate([rank[t : t + 1, :] for t in range(12)], axis=1)
     point = iota((1, POINTS), 1)
-    slot_row = iota((LANES, 1), 0)
+    slot_row = iota((HELD, 1), 0)
     cell = iota((ROWS, 1), 0)
     row_w = jnp.where(cell == rr, along_row0, 0.0) + jnp.where(cell == rr + 1, along_row, 0.0)
     col_w = jnp.where(cell == cc, along_col0, 0.0) + jnp.where(cell == cc + 1, along_col, 0.0)
@@ -157,7 +146,7 @@
         slot = jnp.where(
             (mine_row > 0.0) & (order >= 0) & (order < SLOTS), (point % HUBS) * SLOTS + order, -1
         )
-        chosen = flag01(slot == (slot_row // 8) * SLOTS + slot_row % SLOTS)
+        chosen = flag01(slot == slot_row)
         lhs_ref[...] = dot_t(chosen, row_parts).astype(BF16)
         spread[...] = dot(dot_t(chosen, col_parts).astype(BF16), expand)
 
@@ -194,7 +183,7 @@
         flag01(held(grow - (every // 16) * ROWS, gcol - (every % 16) * COLS)),
         flag01(iota((LANES, 1), 0) == point % HUBS),
     )
-    worst[...] = jnp.broadcast_to(jnp.max(counts), (8, LANES))
+    overfull[0, 0] = jnp.where(jnp.max(counts) > SLOTS, 1, 0)
 
     row_id = iota((ROWS, 1), 0)
     inv_radius = 1.0 / (1.0 + 0.25 * (shell.astype(F32) + 0.5) / 32)
@@ -221,10 +210,8 @@
             spin_dt = spinx[:, pl.ds(off, LANES)] * dt
             base, stretch = [], []
             for f, c in enumerate(fields):
-                up_row = rowrecv[rnd, 0, f : f + 1, pl.ds(off, LANES)] * jnp.where(colat > 0, 1.0, 0.0)
-                down_row = rowrecv[rnd, 1, f : f + 1, pl.ds(off, LANES)] * jnp.where(colat < 7, 1.0, 0.0)
-                n = jnp.where(row_id == 0, up_row, pltpu.roll(c, 1, 0))
-                s = jnp.where(row_id == ROWS - 1, down_row, pltpu.roll(c, ROWS - 1, 0))
+                n = jnp.where(row_id == 0, 0.0, pltpu.roll(c, 1, 0))
+                s = jnp.where(row_id == ROWS - 1, 0.0, pltpu.roll(c, ROWS - 1, 0))
                 w = pltpu.roll(jnp.where(group == 3, tile(f, 0), c), 32, 1)
                 e = pltpu.roll(jnp.where(group == 0, tile(f, 2), c), 96, 1)
                 u = jnp.where(shell == 31, c, pltpu.roll(c, 127, 1))
@@ -248,31 +235,111 @@
                     value = value + add[f]
                 dst[f, :, pl.ds(pl.multiple_of(dst_off + off, LANES), LANES)] = value
 
-    def unpack_halo(rnd):
-        for side, tile, goal in ((0, 0, 3), (1, LANES + WIDTH, 0)):
+    edges = [
+        (colat == 0, lon),
+        (colat == 7, 16 + lon),
+        (lon == 0, 32 + colat),
+        (lon == 15, 40 + colat),
+    ]
+
+    field_id = iota((8, 1), 0)
+    diffuse = jnp.where(field_id < 3, DIFFUSE[0], jnp.where(field_id == 3, DIFFUSE[3], DIFFUSE[6]))
+
+    def add_row(rnd, dst, dst_off, dt, row, sign, values):
+        for t in range(8):
+            tile = slice(LANES + t * LANES, LANES + (t + 1) * LANES)
+            v = values(t)
+            at = ext[rnd, 0, row : row + 1, tile] * (inv_radius * (0.5 * dt * sign))
+            st = ext[rnd, 4, row : row + 1, tile] * (inv_radius * (0.5 * dt * sign))
+            change = (dt * diffuse * (inv_radius * inv_radius) - at) * v + st * pltpu.roll(v, 4, 0)
             for f in range(7):
-                have = colrecv[rnd, side, f // 4]
-                inside = (lon > 0) if side == 0 else (lon < 15)
-                ext[rnd, f, :, tile : tile + LANES] = pltpu.roll(
-                    have, 32 * ((goal - f % 4) % 4), 1
-                ) * jnp.where(inside, 1.0, 0.0)
+                place_at = (f, slice(row, row + 1), slice(dst_off + t * LANES, dst_off + (t + 1) * LANES))
+                dst[place_at] += change[f : f + 1]
+
+    def add_col(rnd, dst, dst_off, dt, t, sign, values):
+        tile = slice(LANES + t * LANES, LANES + (t + 1) * LANES)
+        ap = ext[rnd, 1, :, tile] * (metric_p * (0.5 * dt * sign))
+        sp = ext[rnd, 5, :, tile] * (metric_p * (0.5 * dt * sign))
+        spread_p = metric_p * metric_p * dt
+        vs = [values(f) for f in range(7)]
+        for f in range(7):
+            change = (DIFFUSE[f] * spread_p - ap) * vs[f]
+            if f != 3:
+                change = change + sp * vs[(f + 4) % 8]
+            place_at = (f, slice(None), slice(dst_off + t * LANES, dst_off + (t + 1) * LANES))
+            dst[place_at] += change
+
+    def add_halos(rnd, dst, dst_off, dt):
+        def recv_row(side):
+            return lambda t: rowrecv[rnd, side, :, t * LANES : (t + 1) * LANES]
+
+        def recv_col(side, goal):
+            def values(f):
+                moved = pltpu.roll(colrecv[rnd, side, f // 4], 32 * ((goal - f % 4) % 4), 1)
+                return jnp.where(group == goal, moved, 0.0)
+
+            return values
+
+        pl.when(colat > 0)(lambda: add_row(rnd, dst, dst_off, dt, 0, -1.0, recv_row(0)))
+        pl.when(colat < 7)(lambda: add_row(rnd, dst, dst_off, dt, ROWS - 1, 1.0, recv_row(1)))
+        pl.when(lon > 0)(lambda: add_col(rnd, dst, dst_off, dt, 0, -1.0, recv_col(0, 0)))
+        pl.when(lon < 15)(lambda: add_col(rnd, dst, dst_off, dt, 7, 1.0, recv_col(1, 3)))
+
+    def clear_border(ref, base):
+        for kind, row in ((0, 0), (1, ROWS - 1)):
+
+            @pl.when(edges[kind][0])
+            def _():
+                for f in range(7):
+                    ref[f, row : row + 1, base : base + WIDTH] = jnp.zeros((1, WIDTH), F32)
+
+        for kind, off, goal in ((2, base, 0), (3, base + WIDTH - LANES, 3)):
+
+            @pl.when(edges[kind][0])
+            def _():
+                for f in range(7):
+                    ref[f, :, off : off + LANES] = jnp.where(group == goal, 0.0, ref[f, :, off : off + LANES])
+
+    def add_border(dst, dst_off, dt):
+        def ext_row(row):
+            def values(t):
+                tile = slice(LANES + t * LANES, LANES + (t + 1) * LANES)
+                rows = [ext[1, f, row : row + 1, tile] for f in range(7)]
+                return jnp.concatenate(rows + [jnp.zeros((1, LANES), F32)], axis=0)
+
+            return values
+
+        def ext_col(t, shift, goal):
+            def values(f):
+                have = ext[1, f, :, LANES + t * LANES : LANES + (t + 1) * LANES]
+                return jnp.where(group == goal, pltpu.roll(have, shift, 1), 0.0)
+
+            return values
+
+        pl.when(colat == 0)(lambda: add_row(1, dst, dst_off, dt, 1, -1.0, ext_row(0)))
+        pl.when(colat == 7)(lambda: add_row(1, dst, dst_off, dt, ROWS - 2, 1.0, ext_row(ROWS - 1)))
+        pl.when(lon == 0)(lambda: add_col(1, dst, dst_off, dt, 0, -1.0, ext_col(0, 32, 1)))
+        pl.when(lon == 15)(lambda: add_col(1, dst, dst_off, dt, 7, 1.0, ext_col(7, 96, 2)))
 
     def send_points(ref, base, rnd):
-        row_half = (slot_row % 8) // SLOTS
+        low_rows = iota((8, 1), 0) < SLOTS
 
         def turn_points(turn):
-            total = jnp.zeros((LANES, LANES), F32)
+            halves = [jnp.zeros((HELD, LANES), F32) for _ in range(2)]
             lhs = lhs_ref[...][:, :96]
             for f in range(7):
                 hi, lo = split2(ref[f, :, base : base + WIDTH])
                 rows = dot(lhs, jnp.concatenate([hi, hi, lo], axis=0))
-                folded = jnp.zeros((LANES, LANES), F32)
+                folded = jnp.zeros((HELD, LANES), F32)
                 for t in range(8):
                     folded += rows[:, t * LANES : (t + 1) * LANES] * spread[:, t * LANES : (t + 1) * LANES]
                 folded += pltpu.roll(folded, 32, 1)
                 folded += pltpu.roll(folded, 64, 1)
-                total = jnp.where((group == f % 4) & (row_half == f // 4), folded, total)
-            p1send[rnd, turn] = total.reshape(HUBS, 8, LANES)
+                halves[f // 4] = jnp.where(group == f % 4, folded, halves[f // 4])
+            for v in range(HUBS // 2):
+                first, second = (part[8 * v : 8 * v + 8] for part in halves)
+                p1send[rnd, turn, 2 * v] = jnp.where(low_rows, first, pltpu.roll(second, SLOTS, 0))
+                p1send[rnd, turn, 2 * v + 1] = jnp.where(low_rows, pltpu.roll(first, SLOTS, 0), second)
             p1recv[rnd, turn, hub] = p1send[rnd, turn, hub]
 
             @pl.loop(1, HUBS)
@@ -335,13 +402,6 @@
         def _(i):
             send(32 + i, 2, i, 0)
             send(40 + i, 3, i, 15)
-
-    edges = [
-        (colat == 0, lon),
-        (colat == 7, 16 + lon),
-        (lon == 0, 32 + colat),
-        (lon == 15, 40 + colat),
-    ]
 
     def place(rnd, ref, base):
         line = iota((64, 1), 0)
@@ -359,7 +419,7 @@
                 for h in range(HUBS):
                     summed[4 * h : 4 * h + 4, :] = total[h]
                 x = summed[...]
-                own = angle[:, pl.ds(pl.multiple_of((segment // 4) * LANES, LANES), LANES)]
+                own = angle[pl.ds(pl.multiple_of((segment // 4) * LANES, LANES), LANES)].reshape(1, LANES)
                 own = jnp.where(lane == (segment % 4) * 32 + line_point, own, 0.0)
                 own = jnp.sum(own, axis=1, keepdims=True)
                 cosine, sine = jnp.cos(own), jnp.sin(own)
@@ -391,21 +451,38 @@
 
     for f in range(7):
         ext[0, f, :, LANES : LANES + WIDTH] = state[f]
+        for rnd in range(2):
+            ext[rnd, f, :, :LANES] = jnp.zeros((ROWS, LANES), F32)
+            ext[rnd, f, :, LANES + WIDTH :] = jnp.zeros((ROWS, LANES), F32)
+    pack_halo(state, 0, 0)
+    pl.semaphore_wait(barrier, 31 + 7 + 2)
+    halos0 = halo_copies(0)
+    for copy in halos0:
+        copy.start()
+
+    @pl.loop(1, 8)
+    def _(f):
+        pl.semaphore_signal(
+            ready, inc=1, device_id=dict(lon=((plane + f) % 8) * 2 + y_lo), device_id_type=MESH
+        )
+
+    rate(0, state, 0, ext.at[1], LANES, 0.1)
     for copy in halos0:
         copy.wait_recv()
-    unpack_halo(0)
-    rate(0, state, 0, ext.at[1], LANES, 0.1)
+    add_halos(0, ext.at[1], LANES, 0.1)
+    clear_border(ext.at[1], LANES)
     send_points(ext.at[1], LANES, 0)
     pack_halo(ext.at[1], LANES, 1)
     halos1 = halo_copies(1)
     for copy in halos1:
         copy.start()
     relay(0)
+    rate(1, state, 0, out, 0, 0.2)
     for copy in halos1:
         copy.wait_recv()
-    unpack_halo(1)
+    add_halos(1, out, 0, 0.2)
     place(0, ext.at[1], LANES)
-    rate(1, state, 0, out, 0, 0.2)
+    add_border(out, 0, 0.2)
     send_points(out, 0, 1)
     relay(1)
     place(1, out, 0)
@@ -424,10 +501,10 @@
         functools.partial(step_kernel, rounds),
         out_shape=(
             jax.ShapeDtypeStruct((7, ROWS, WIDTH), F32),
-            jax.ShapeDtypeStruct((8, LANES), F32),
+            jax.ShapeDtypeStruct((1, 1), I32),
         ),
         in_specs=[vmem] * 7,
-        out_specs=(vmem, vmem),
+        out_specs=(vmem, pl.BlockSpec(memory_space=pltpu.SMEM)),
         scratch_shapes=[
             scratch(2, 7, ROWS, WIDTH + 2 * LANES),
             scratch(2, 2, 8, WIDTH),
@@ -439,9 +516,9 @@
             scratch(2, SEGMENTS, 4, LANES),
             scratch(2, 4, 8 * HUBS, 4, LANES),
             scratch(64, LANES),
-            scratch(LANES, WIDTH),
+            scratch(HELD, WIDTH),
             scratch(ROWS, WIDTH),
-            pltpu.VMEM((LANES, LANES), BF16),
+            pltpu.VMEM((HELD, LANES), BF16),
             pltpu.VMEM((192, LANES), BF16),
             scratch(192, LANES),
             pltpu.SemaphoreType.DMA((2, 4)),
@@ -460,10 +537,10 @@
 
 
 def on_device(state, spin, donor_device, donor_row, donor_col, corner_weights, border_angle):
-    args = (state[0], spin, donor_device, donor_row, donor_col, corner_weights, border_angle[None])
-    fast, worst = step(1, *args)
+    args = (state[0], spin, donor_device, donor_row, donor_col, corner_weights, border_angle)
+    fast, overfull = step(1, *args)
     turns = POINTS // HUBS // SLOTS
-    advanced = lax.cond(worst[0, 0] > SLOTS, lambda: step(turns, *args)[0], lambda: fast)
+    advanced = lax.cond(overfull[0, 0] > 0, lambda: step(turns, *args)[0], lambda: fast)
     return advanced[None]
 
 

time: 53.1 us -> 48.5 us (0.913)
  Pallas kernels: 50 us -> 46.7 us
  local copies, waits for them, and re-layouts: 2.25 us -> 0.95 us
    pallas_call x1, Pallas kernels: 50 us -> 46.7 us  [step(): pl.pallas_call(functools.partial(step_kernel, rounds), out_shape=(jax.Sha...]
    broadcast_in_dim x1 -> x0, local copies, waits for them, and re-layouts: 0.78 us -> none  [on_device(): border_angle[None]]
where the time goes in v3:
time: 48.5 us; the launch traced here: 48.4 us
  Pallas kernels  46.7 us (96%)
  local copies, waits for them, and re-layouts  0.95 us (2%)
  between operations  0.74 us (2%)
    pallas_call x1, Pallas kernels, step(): pl.pallas_call(functools.partial(step_kernel, rounds), out_shape=(jax.Sha...  46.7 us

profile of v3, /device:TPU:1, one launch (start us, length us, event | category | flops | bytes accessed | tf_op | source)
XLA Modules:
  0.0 48.4 jit_solution(16244927542068549846)
XLA Ops:
  0.0 0.0 copy-start
  0.0 0.0 copy-start.1
  0.0 0.0 copy-start.2
  0.0 0.0 copy-start.3
  0.0 0.0 copy-start.4
  0.0 0.0 copy-start.5
  0.0 0.0 copy-start.6
  0.0 46.7 %dynamo_step.1 = (f32[7,32,1024]{2,1,0:T(8,128)S(1)}, s32[1,1]{1,0:T(1,128)}) custom-call(f32[7,32,1024]{2,1,0:T(8,128)} %bitcast.4, f32[1,32,32]{2,1,0:T(8,128)} %spin.1, s32[4,1536]{1,0:T(4,128)} %device.1, s32[4,1536]{1,0:T(4,128)} %drow.1, s32[4,1536]{1,0:T(4,128)} %dcol.1, f32[4,1536]{1,0:T(4,128)} %weights.1, f32[1536]{0:T(1024)} %angle.1), custom_call_target="tpu_custom_call" | custom-call | tf_op jit(solution)/shard_map/dynamo_step/pallas_call | solution.py:500
  47.4 0.0 copy-done
  47.4 0.0 copy-done.1
  47.4 0.0 copy-done.2
  47.5 0.0 copy-done.3
  47.5 0.0 copy-done.4
  47.5 0.0 copy-done.5
  47.5 0.0 copy-done.6
  47.5 0.9 %copy.14 = f32[1,7,32,1024]{3,2,1,0:T(8,128)} copy(f32[1,7,32,1024]{3,2,1,0:T(8,128)S(1)} %get-tuple-element.37) | data formatting | bytes 1835008
  (1 shorter events, 0.0 us)
Async XLA Ops:
  0.0 47.4 %copy-start = (f32[1,7,32,1024]{3,2,1,0:T(8,128)S(1)}, f32[1,7,32,1024]{3,2,1,0:T(8,128)}, u32[]{:S(2)}) copy-start(f32[1,7,32,1024]{3,2,1,0:T(8,128)} %param.9) | copy-start | bytes 2752516
  0.0 47.4 %copy-start.1 = (s32[4,1536]{1,0:T(4,128)S(1)}, s32[4,1536]{1,0:T(4,128)}, u32[]{:S(2)}) copy-start(s32[4,1536]{1,0:T(4,128)} %device.1) | copy-start | bytes 73732
  0.0 47.4 %copy-start.2 = (s32[4,1536]{1,0:T(4,128)S(1)}, s32[4,1536]{1,0:T(4,128)}, u32[]{:S(2)}) copy-start(s32[4,1536]{1,0:T(4,128)} %drow.1) | copy-start | bytes 73732
  0.0 47.5 %copy-start.3 = (s32[4,1536]{1,0:T(4,128)S(1)}, s32[4,1536]{1,0:T(4,128)}, u32[]{:S(2)}) copy-start(s32[4,1536]{1,0:T(4,128)} %dcol.1) | copy-start | bytes 73732
  0.0 47.5 %copy-start.4 = (f32[4,1536]{1,0:T(4,128)S(1)}, f32[4,1536]{1,0:T(4,128)}, u32[]{:S(2)}) copy-start(f32[4,1536]{1,0:T(4,128)} %weights.1) | copy-start | bytes 73732
  0.0 47.5 %copy-start.5 = (f32[1,32,32]{2,1,0:T(8,128)S(1)}, f32[1,32,32]{2,1,0:T(8,128)}, u32[]{:S(2)}) copy-start(f32[1,32,32]{2,1,0:T(8,128)} %spin.1) | copy-start | bytes 12292
  0.0 47.5 %copy-start.6 = (f32[1536]{0:T(1024)S(1)}, f32[1536]{0:T(1024)}, u32[]{:S(2)}) copy-start(f32[1536]{0:T(1024)} %angle.1) | copy-start | bytes 18436

commit v4 on v3

--- a/solution.py
+++ b/solution.py
@@ -11,7 +11,8 @@
 F32, BF16, I32 = jnp.float32, jnp.bfloat16, jnp.int32
 ROWS, COLS, WIDTH, LANES = 32, 32, 1024, 128
 HELD = 64
-POINTS, HUBS, SLOTS, SEGMENTS = 1536, 16, 4, 48
+POINTS, HUBS, SLOTS, SEGMENTS = 1536, 32, 2, 48
+PARCEL = 2 * SLOTS
 DIFFUSE = (0.3, 0.3, 0.3, 0.4, 0.5, 0.5, 0.5)
 
 
@@ -47,11 +48,12 @@
     rounds,
     state, spin, device, drow, dcol, weights, angle, out, overfull,
     ext, rowsend, rowrecv, colsend, colrecv, p1send, p1recv, p2send, p2recv, summed, spread, spinx,
-    lhs_ref, pick_ref, hub_sum, halo_ss, halo_rs, p1_ss, p1_rs, p2_ss, p2_rs, ready,
+    lhs_ref, pick_ref, hub_sum, halo_ss, halo_rs, p1_ss, p1_rs, p2_ss, p2_rs, state_sem, ready, all_in,
 ):
     panel, colat, lon = (lax.axis_index(a) for a in ("panel", "colat", "lon"))
     plane, y_lo = lon // 2, lon % 2
-    hub = colat * 2 + y_lo
+    pair, odd = plane // 2, plane % 2
+    hub = (colat * 2 + y_lo) * 2 + odd
     other = 1 - panel
 
     barrier = pltpu.get_barrier_semaphore()
@@ -60,18 +62,23 @@
         pl.semaphore_signal(barrier, inc=1, device_id=where, device_id_type=MESH)
 
     def peer(h):
-        return dict(colat=h // 2, lon=plane * 2 + h % 2)
-
-    @pl.loop(1, 32)
+        return dict(colat=h // 4, lon=(pair * 2 + h % 2) * 2 + (h // 2) % 2)
+
+    def across(f):
+        return dict(lon=(((pair + f) % 4) * 2 + odd) * 2 + y_lo)
+
+    whole_state = pltpu.make_async_copy(state, ext.at[0, :, :, pl.ds(LANES, WIDTH)], state_sem)
+    whole_state.start()
+
+    @pl.loop(1, HUBS)
     def _(f):
-        t = (panel * 16 + hub + f) % 32
-        h = t % 16
-        greet(panel=t // 16, colat=h // 2, lon=plane * 2 + h % 2)
-
-    @pl.loop(1, 8)
+        greet(**peer((hub + f) % HUBS))
+
+    @pl.loop(1, 4)
     def _(f):
-        greet(lon=((plane + f) % 8) * 2 + y_lo)
-
+        greet(**across(f))
+
+    greet(panel=other)
     north, south = (colat + 7) % 8, (colat + 1) % 8
     west, east = (lon + 15) % 16, (lon + 1) % 16
     greet(lon=west)
@@ -153,25 +160,26 @@
     spin_parts = jnp.concatenate(list(split3(spin[0])) + [jnp.zeros((ROWS, COLS), BF16)], axis=1)
     spinx[...] = dot(spin_parts, expand)
 
-    out_row = iota((192, 1), 0)
-    my_lane = ((out_row // 2) % 8) * HUBS + hub
+    out_row = iota((2 * SEGMENTS, 1), 0)
+    my_lane = ((out_row // 2) % 4) * HUBS + hub
 
     def column(values):
         tall = jnp.concatenate(
-            [jnp.broadcast_to(values[:, t * LANES : (t + 1) * LANES], (16, LANES)) for t in range(12)], axis=0
+            [jnp.broadcast_to(values[:, t * LANES : (t + 1) * LANES], (8, LANES)) for t in range(12)], axis=0
         )
         return jnp.sum(jnp.where(lane == my_lane, tall, 0), axis=1, keepdims=True)
 
-    source = lane // 8
-    s_rr = column(grow) - (source // 2) * ROWS
-    s_cc = column(gcol) - (plane * 2 + source % 2) * COLS
+    parcel_lane = iota((1, HUBS * PARCEL), 1)
+    source = parcel_lane // PARCEL
+    s_rr = column(grow) - (source // 4) * ROWS
+    s_cc = column(gcol) - ((pair * 2 + source % 2) * 2 + (source // 2) % 2) * COLS
     has = held(s_rr, s_cc)
-    count_row, count_col = iota((192, 192), 0), iota((192, 192), 1)
+    count_row, count_col = (iota((2 * SEGMENTS, 2 * SEGMENTS), d) for d in range(2))
     seen = dot(flag01((count_col // 2 < count_row // 2) & (count_col % 2 == 0)), flag01(has))
 
     def fill_picks(turn):
         slot = seen.astype(I32) - turn * SLOTS
-        take = has & (slot == lane % SLOTS) & (out_row % 2 == (lane % 8) // SLOTS)
+        take = has & (slot == parcel_lane % SLOTS) & (out_row % 2 == (parcel_lane % PARCEL) // SLOTS)
         pick_ref[...] = flag01(take)
 
     if rounds == 1:
@@ -322,8 +330,6 @@
         pl.when(lon == 15)(lambda: add_col(1, dst, dst_off, dt, 7, 1.0, ext_col(7, 96, 2)))
 
     def send_points(ref, base, rnd):
-        low_rows = iota((8, 1), 0) < SLOTS
-
         def turn_points(turn):
             halves = [jnp.zeros((HELD, LANES), F32) for _ in range(2)]
             lhs = lhs_ref[...][:, :96]
@@ -336,10 +342,11 @@
                 folded += pltpu.roll(folded, 32, 1)
                 folded += pltpu.roll(folded, 64, 1)
                 halves[f // 4] = jnp.where(group == f % 4, folded, halves[f // 4])
-            for v in range(HUBS // 2):
-                first, second = (part[8 * v : 8 * v + 8] for part in halves)
-                p1send[rnd, turn, 2 * v] = jnp.where(low_rows, first, pltpu.roll(second, SLOTS, 0))
-                p1send[rnd, turn, 2 * v + 1] = jnp.where(low_rows, pltpu.roll(first, SLOTS, 0), second)
+            for h in range(HUBS):
+                for half in range(2):
+                    p1send[rnd, turn, h, half * SLOTS : (half + 1) * SLOTS, :] = halves[half][
+                        h * SLOTS : (h + 1) * SLOTS
+                    ]
             p1recv[rnd, turn, hub] = p1send[rnd, turn, hub]
 
             @pl.loop(1, HUBS)
@@ -366,7 +373,7 @@
     def relay(rnd):
         def turn_sum(turn):
             wait_bytes(p1recv.at[rnd, turn, pl.ds(0, HUBS - 1)], p1_rs.at[rnd, turn])
-            parts = jnp.concatenate(split3(p1recv[rnd, turn].reshape(LANES, LANES)), axis=0)
+            parts = jnp.concatenate(split3(p1recv[rnd, turn].reshape(HUBS * PARCEL, LANES)), axis=0)
             pick = pick_ref[...]
             return dot(jnp.concatenate([pick, pick, pick], axis=1), parts)
 
@@ -382,13 +389,13 @@
 
             picked = hub_sum[...]
         for s in range(SEGMENTS):
-            p2send[rnd, s] = picked[4 * s : 4 * s + 4, :]
+            p2send[rnd, s] = picked[2 * s : 2 * s + 2, :]
         if rnd == 0:
-            pl.semaphore_wait(ready, 7)
+            pl.semaphore_wait(all_in, 1)
 
         def send(s, kind, to_colat, to_lon):
             pltpu.make_async_remote_copy(
-                src_ref=p2send.at[rnd, s], dst_ref=p2recv.at[rnd, kind, plane * HUBS + hub],
+                src_ref=p2send.at[rnd, s], dst_ref=p2recv.at[rnd, kind, pair * HUBS + hub],
                 send_sem=p2_ss.at[rnd], recv_sem=p2_rs.at[rnd, kind],
                 device_id=dict(panel=other, colat=to_colat, lon=to_lon), device_id_type=MESH,
             ).start()
@@ -405,7 +412,7 @@
 
     def place(rnd, ref, base):
         line = iota((64, 1), 0)
-        line_point = 16 * ((line // 2) % 2) + line // 4
+        line_point = line // 2
         from_row = iota((64, 64), 0)
         from_col = iota((64, 64), 1)
         for kind, (here, segment) in enumerate(edges):
@@ -414,10 +421,10 @@
             def _():
                 wait_bytes(p2recv.at[rnd, kind], p2_rs.at[rnd, kind])
                 total = p2recv[rnd, kind, 0:HUBS]
-                for z in range(1, 8):
+                for z in range(1, 4):
                     total = total + p2recv[rnd, kind, z * HUBS : (z + 1) * HUBS]
                 for h in range(HUBS):
-                    summed[4 * h : 4 * h + 4, :] = total[h]
+                    summed[2 * h : 2 * h + 2, :] = total[h]
                 x = summed[...]
                 own = angle[pl.ds(pl.multiple_of((segment // 4) * LANES, LANES), LANES)].reshape(1, LANES)
                 own = jnp.where(lane == (segment % 4) * 32 + line_point, own, 0.0)
@@ -429,7 +436,7 @@
                 part = from_row // 32
                 at = from_row % 32
                 j = at if kind >= 2 else 4 * (at % 8) + at // 8
-                perm = flag01(from_col == 4 * (j % 16) + 2 * (j // 16) + part)
+                perm = flag01(from_col == 2 * j + part)
                 x = dot(jnp.concatenate([perm, perm, perm], axis=1), jnp.concatenate(split3(x), axis=0))
                 for f in range(7):
                     block = x[32 * (f // 4) : 32 * (f // 4) + 32]
@@ -450,34 +457,34 @@
                         ref[f, :, off : off + LANES] = jnp.where(group == goal, blend, now)
 
     for f in range(7):
-        ext[0, f, :, LANES : LANES + WIDTH] = state[f]
         for rnd in range(2):
             ext[rnd, f, :, :LANES] = jnp.zeros((ROWS, LANES), F32)
             ext[rnd, f, :, LANES + WIDTH :] = jnp.zeros((ROWS, LANES), F32)
-    pack_halo(state, 0, 0)
-    pl.semaphore_wait(barrier, 31 + 7 + 2)
+    whole_state.wait()
+    pack_halo(ext.at[0], LANES, 0)
+    pl.semaphore_wait(barrier, 31 + 3 + 1 + 2)
     halos0 = halo_copies(0)
     for copy in halos0:
         copy.start()
 
-    @pl.loop(1, 8)
+    @pl.loop(1, 4)
     def _(f):
-        pl.semaphore_signal(
-            ready, inc=1, device_id=dict(lon=((plane + f) % 8) * 2 + y_lo), device_id_type=MESH
-        )
-
-    rate(0, state, 0, ext.at[1], LANES, 0.1)
+        pl.semaphore_signal(ready, inc=1, device_id=across(f), device_id_type=MESH)
+
+    rate(0, ext.at[0], LANES, ext.at[1], LANES, 0.1)
     for copy in halos0:
         copy.wait_recv()
     add_halos(0, ext.at[1], LANES, 0.1)
     clear_border(ext.at[1], LANES)
     send_points(ext.at[1], LANES, 0)
+    pl.semaphore_wait(ready, 3)
+    pl.semaphore_signal(all_in, inc=1, device_id=dict(panel=other), device_id_type=MESH)
     pack_halo(ext.at[1], LANES, 1)
     halos1 = halo_copies(1)
     for copy in halos1:
         copy.start()
     relay(0)
-    rate(1, state, 0, out, 0, 0.2)
+    rate(1, ext.at[0], LANES, out, 0, 0.2)
     for copy in halos1:
         copy.wait_recv()
     add_halos(1, out, 0, 0.2)
@@ -503,7 +510,7 @@
             jax.ShapeDtypeStruct((7, ROWS, WIDTH), F32),
             jax.ShapeDtypeStruct((1, 1), I32),
         ),
-        in_specs=[vmem] * 7,
+        in_specs=[pl.BlockSpec(memory_space=pl.ANY)] + [vmem] * 6,
         out_specs=(vmem, pl.BlockSpec(memory_space=pltpu.SMEM)),
         scratch_shapes=[
             scratch(2, 7, ROWS, WIDTH + 2 * LANES),
@@ -511,22 +518,24 @@
             scratch(2, 2, 8, WIDTH),
             scratch(2, 2, 2, ROWS, LANES),
             scratch(2, 2, 2, ROWS, LANES),
-            scratch(2, rounds, HUBS, 8, LANES),
-            scratch(2, rounds, HUBS, 8, LANES),
-            scratch(2, SEGMENTS, 4, LANES),
-            scratch(2, 4, 8 * HUBS, 4, LANES),
+            scratch(2, rounds, HUBS, PARCEL, LANES),
+            scratch(2, rounds, HUBS, PARCEL, LANES),
+            scratch(2, SEGMENTS, 2, LANES),
+            scratch(2, 4, 4 * HUBS, 2, LANES),
             scratch(64, LANES),
             scratch(HELD, WIDTH),
             scratch(ROWS, WIDTH),
             pltpu.VMEM((HELD, LANES), BF16),
-            pltpu.VMEM((192, LANES), BF16),
-            scratch(192, LANES),
+            pltpu.VMEM((2 * SEGMENTS, HUBS * PARCEL), BF16),
+            scratch(2 * SEGMENTS, LANES),
             pltpu.SemaphoreType.DMA((2, 4)),
             pltpu.SemaphoreType.DMA((2, 4)),
             pltpu.SemaphoreType.DMA((2, rounds)),
             pltpu.SemaphoreType.DMA((2, rounds)),
             pltpu.SemaphoreType.DMA((2,)),
             pltpu.SemaphoreType.DMA((2, 4)),
+            pltpu.SemaphoreType.DMA,
+            pltpu.SemaphoreType.REGULAR,
             pltpu.SemaphoreType.REGULAR,
         ],
         compiler_params=pltpu.CompilerParams(

time: 48.5 us -> 44.9 us (0.926)
  Pallas kernels: 46.7 us -> 43 us
    pallas_call x1, Pallas kernels: 46.7 us -> 43 us  [step(): pl.pallas_call(functools.partial(step_kernel, rounds), out_shape=(jax.Sha...]
where the time goes in v4:
time: 44.9 us; the launch traced here: 44.7 us
  Pallas kernels  43 us (96%)
  local copies, waits for them, and re-layouts  0.95 us (2%)
  between operations  0.74 us (2%)
    pallas_call x1, Pallas kernels, step(): pl.pallas_call(functools.partial(step_kernel, rounds), out_shape=(jax.Sha...  43 us
    unnamed x15, local copies, waits for them, and re-layouts  0.95 us

profile of v4, /device:TPU:1, one launch (start us, length us, event | category | flops | bytes accessed | tf_op | source)
XLA Modules:
  0.0 44.7 jit_solution(10743208250182156057)
XLA Ops:
  0.0 0.0 copy-start
  0.0 0.0 copy-start.1
  0.0 0.0 copy-start.2
  0.0 0.0 copy-start.3
  0.0 0.0 copy-start.4
  0.0 0.0 copy-start.5
  0.0 0.0 copy-start.6
  0.0 43.0 %dynamo_step.1 = (f32[7,32,1024]{2,1,0:T(8,128)S(1)}, s32[1,1]{1,0:T(1,128)}) custom-call(f32[7,32,1024]{2,1,0:T(8,128)} %bitcast.4, f32[1,32,32]{2,1,0:T(8,128)} %spin.1, s32[4,1536]{1,0:T(4,128)} %device.1, s32[4,1536]{1,0:T(4,128)} %drow.1, s32[4,1536]{1,0:T(4,128)} %dcol.1, f32[4,1536]{1,0:T(4,128)} %weights.1, f32[1536]{0:T(1024)} %angle.1), custom_call_target="tpu_custom_call" | custom-call | tf_op jit(solution)/shard_map/dynamo_step/pallas_call | solution.py:507
  43.7 0.0 copy-done
  43.7 0.0 copy-done.1
  43.8 0.0 copy-done.2
  43.8 0.0 copy-done.3
  43.8 0.0 copy-done.4
  43.8 0.0 copy-done.5
  43.8 0.0 copy-done.6
  43.8 0.9 %copy.14 = f32[1,7,32,1024]{3,2,1,0:T(8,128)} copy(f32[1,7,32,1024]{3,2,1,0:T(8,128)S(1)} %get-tuple-element.37) | data formatting | bytes 1835008
  (1 shorter events, 0.0 us)
Async XLA Ops:
  0.0 43.7 %copy-start = (f32[1,7,32,1024]{3,2,1,0:T(8,128)S(1)}, f32[1,7,32,1024]{3,2,1,0:T(8,128)}, u32[]{:S(2)}) copy-start(f32[1,7,32,1024]{3,2,1,0:T(8,128)} %param.9) | copy-start | bytes 2752516
  0.0 43.7 %copy-start.1 = (s32[4,1536]{1,0:T(4,128)S(1)}, s32[4,1536]{1,0:T(4,128)}, u32[]{:S(2)}) copy-start(s32[4,1536]{1,0:T(4,128)} %device.1) | copy-start | bytes 73732
  0.0 43.8 %copy-start.2 = (s32[4,1536]{1,0:T(4,128)S(1)}, s32[4,1536]{1,0:T(4,128)}, u32[]{:S(2)}) copy-start(s32[4,1536]{1,0:T(4,128)} %drow.1) | copy-start | bytes 73732
  0.0 43.8 %copy-start.3 = (s32[4,1536]{1,0:T(4,128)S(1)}, s32[4,1536]{1,0:T(4,128)}, u32[]{:S(2)}) copy-start(s32[4,1536]{1,0:T(4,128)} %dcol.1) | copy-start | bytes 73732
  0.0 43.8 %copy-start.4 = (f32[4,1536]{1,0:T(4,128)S(1)}, f32[4,1536]{1,0:T(4,128)}, u32[]{:S(2)}) copy-start(f32[4,1536]{1,0:T(4,128)} %weights.1) | copy-start | bytes 73732
  0.0 43.8 %copy-start.5 = (f32[1,32,32]{2,1,0:T(8,128)S(1)}, f32[1,32,32]{2,1,0:T(8,128)}, u32[]{:S(2)}) copy-start(f32[1,32,32]{2,1,0:T(8,128)} %spin.1) | copy-start | bytes 12292
  0.0 43.8 %copy-start.6 = (f32[1536]{0:T(1024)S(1)}, f32[1536]{0:T(1024)}, u32[]{:S(2)}) copy-start(f32[1536]{0:T(1024)} %angle.1) | copy-start | bytes 18436

commit v5 on v4

--- a/solution.py
+++ b/solution.py
@@ -10,9 +10,9 @@
 MESH = pl.DeviceIdType.MESH
 F32, BF16, I32 = jnp.float32, jnp.bfloat16, jnp.int32
 ROWS, COLS, WIDTH, LANES = 32, 32, 1024, 128
-HELD = 64
-POINTS, HUBS, SLOTS, SEGMENTS = 1536, 32, 2, 48
-PARCEL = 2 * SLOTS
+POINTS, HUBS, SLOTS, PARCEL = 1536, 32, 3, 8
+HELD = HUBS * SLOTS
+SERVED = 24
 DIFFUSE = (0.3, 0.3, 0.3, 0.4, 0.5, 0.5, 0.5)
 
 
@@ -46,14 +46,15 @@
 
 def step_kernel(
     rounds,
-    state, spin, device, drow, dcol, weights, angle, out, overfull,
-    ext, rowsend, rowrecv, colsend, colrecv, p1send, p1recv, p2send, p2recv, summed, spread, spinx,
-    lhs_ref, pick_ref, hub_sum, halo_ss, halo_rs, p1_ss, p1_rs, p2_ss, p2_rs, state_sem, ready, all_in,
+    state, spin_in, device_in, drow_in, dcol_in, weights_in, angle_in, out, overfull,
+    spin, device, drow, dcol, weights, angle, turn_cos, turn_sin, ext, rowsend, rowrecv, colsend, colrecv, p1send, p1recv, p2send, p2recv, summed, spread, spinx,
+    lhs_ref, pick_ref, hub_sum, halo_ss, halo_rs, p1_ss, p1_rs, p2_ss, p2_rs, state_sem, table_sems, ready, all_in,
 ):
     panel, colat, lon = (lax.axis_index(a) for a in ("panel", "colat", "lon"))
     plane, y_lo = lon // 2, lon % 2
     pair, odd = plane // 2, plane % 2
-    hub = (colat * 2 + y_lo) * 2 + odd
+    mix = colat * 2 + odd
+    hub = y_lo * 16 + mix
     other = 1 - panel
 
     barrier = pltpu.get_barrier_semaphore()
@@ -62,13 +63,27 @@
         pl.semaphore_signal(barrier, inc=1, device_id=where, device_id_type=MESH)
 
     def peer(h):
-        return dict(colat=h // 4, lon=(pair * 2 + h % 2) * 2 + (h // 2) % 2)
+        return dict(colat=(h % 16) // 2, lon=(pair * 2 + h % 2) * 2 + h // 16)
 
     def across(f):
         return dict(lon=(((pair + f) % 4) * 2 + odd) * 2 + y_lo)
 
     whole_state = pltpu.make_async_copy(state, ext.at[0, :, :, pl.ds(LANES, WIDTH)], state_sem)
+    tables = [
+        pltpu.make_async_copy(source, target, table_sems.at[i])
+        for i, (source, target) in enumerate(
+            zip(
+                (device_in, drow_in, dcol_in, weights_in, spin_in, angle_in),
+                (device, drow, dcol, weights, spin, angle),
+                strict=True,
+            )
+        )
+    ]
+    for copy in tables[:4]:
+        copy.start()
     whole_state.start()
+    for copy in tables[4:]:
+        copy.start()
 
     @pl.loop(1, HUBS)
     def _(f):
@@ -115,6 +130,8 @@
             copy(colsend.at[rnd, 1], colrecv.at[rnd, 0], 3, lon=east),
         ]
 
+    for copy in tables:
+        copy.wait()
     grow = (device[0:1, :] // 16) * ROWS + drow[0:1, :]
     gcol = (device[0:1, :] % 16) * COLS + dcol[0:1, :]
     along_row = weights[1:2, :] + weights[3:4, :]
@@ -127,16 +144,23 @@
 
     rr, cc = grow - colat * ROWS, gcol - lon * COLS
     mine_row = jnp.where(held(rr, cc), 1.0, 0.0)
-    mine = jnp.concatenate([mine_row[:, t * LANES : (t + 1) * LANES] for t in range(12)], axis=0)
-    mine = jnp.concatenate([mine, jnp.zeros((4, LANES), F32)], axis=0).astype(BF16)
+    point = iota((1, POINTS), 1)
+    segment_of = point // 32
+    side = jnp.where(segment_of < 32, 1 - segment_of % 2, jnp.where(segment_of < 40, 1, 0))
+    point_hub = side * 16 + point % 16
+    lists = []
+    for y in range(2):
+        part = jnp.where(side == y, mine_row, 0.0)
+        lists += [part[:, t * LANES : (t + 1) * LANES] for t in range(12)] + [jnp.zeros((4, LANES), F32)]
+    lists = jnp.concatenate(lists, axis=0).astype(BF16)
     up, down = iota((LANES, LANES), 0), iota((LANES, LANES), 1)
-    same = up % HUBS == down % HUBS
-    before = dot(mine, flag01(same & (up < down)))
-    whole = dot(mine, flag01(same)).astype(BF16)
-    earlier = dot(flag01(iota((16, 16), 0) > iota((16, 16), 1)), whole)
-    rank = before + earlier
-    rank_row = jnp.concatenate([rank[t : t + 1, :] for t in range(12)], axis=1)
-    point = iota((1, POINTS), 1)
+    same = up % 16 == down % 16
+    before = dot(lists, flag01(same & (up < down)))
+    whole = dot(lists, flag01(same)).astype(BF16)
+    up, down = iota((32, 32), 0), iota((32, 32), 1)
+    rank = before + dot(flag01((up > down) & (up // 16 == down // 16)), whole)
+    ranks = [jnp.concatenate([rank[16 * y + t : 16 * y + t + 1, :] for t in range(12)], axis=1) for y in range(2)]
+    rank_row = jnp.where(side == 0, ranks[0], ranks[1])
     slot_row = iota((HELD, 1), 0)
     cell = iota((ROWS, 1), 0)
     row_w = jnp.where(cell == rr, along_row0, 0.0) + jnp.where(cell == rr + 1, along_row, 0.0)
@@ -151,7 +175,7 @@
     def fill_slots(turn):
         order = rank_row.astype(I32) - turn * SLOTS
         slot = jnp.where(
-            (mine_row > 0.0) & (order >= 0) & (order < SLOTS), (point % HUBS) * SLOTS + order, -1
+            (mine_row > 0.0) & (order >= 0) & (order < SLOTS), point_hub * SLOTS + order, -1
         )
         chosen = flag01(slot == slot_row)
         lhs_ref[...] = dot_t(chosen, row_parts).astype(BF16)
@@ -160,26 +184,30 @@
     spin_parts = jnp.concatenate(list(split3(spin[0])) + [jnp.zeros((ROWS, COLS), BF16)], axis=1)
     spinx[...] = dot(spin_parts, expand)
 
-    out_row = iota((2 * SEGMENTS, 1), 0)
-    my_lane = ((out_row // 2) % 4) * HUBS + hub
+    out_row = iota((4 * SERVED, 1), 0)
+    served = out_row // 4
+    quarter = jnp.where(served < 16, 2 * (served % 2) + 1 - y_lo, served % 4)
+    my_lane = 32 * quarter + 16 * ((out_row // 2) % 2) + colat * 2 + odd
 
     def column(values):
-        tall = jnp.concatenate(
-            [jnp.broadcast_to(values[:, t * LANES : (t + 1) * LANES], (8, LANES)) for t in range(12)], axis=0
-        )
-        return jnp.sum(jnp.where(lane == my_lane, tall, 0), axis=1, keepdims=True)
+        tiles = [values[:, t * LANES : (t + 1) * LANES] for t in range(12)]
+        tall = [jnp.broadcast_to(tile, (8, LANES)) for tile in tiles[:8]]
+        tall += [
+            jnp.broadcast_to(jnp.where(y_lo == 1, tiles[8 + i], tiles[10 + i]), (16, LANES)) for i in range(2)
+        ]
+        return jnp.sum(jnp.where(lane == my_lane, jnp.concatenate(tall, axis=0), 0), axis=1, keepdims=True)
 
     parcel_lane = iota((1, HUBS * PARCEL), 1)
     source = parcel_lane // PARCEL
-    s_rr = column(grow) - (source // 4) * ROWS
-    s_cc = column(gcol) - ((pair * 2 + source % 2) * 2 + (source // 2) % 2) * COLS
+    s_rr = column(grow) - ((source % 16) // 2) * ROWS
+    s_cc = column(gcol) - ((pair * 2 + source % 2) * 2 + source // 16) * COLS
     has = held(s_rr, s_cc)
-    count_row, count_col = (iota((2 * SEGMENTS, 2 * SEGMENTS), d) for d in range(2))
+    count_row, count_col = (iota((4 * SERVED, 4 * SERVED), d) for d in range(2))
     seen = dot(flag01((count_col // 2 < count_row // 2) & (count_col % 2 == 0)), flag01(has))
 
     def fill_picks(turn):
         slot = seen.astype(I32) - turn * SLOTS
-        take = has & (slot == parcel_lane % SLOTS) & (out_row % 2 == (parcel_lane % PARCEL) // SLOTS)
+        take = has & (slot == parcel_lane % 4) & (slot < SLOTS) & (out_row % 2 == (parcel_lane % PARCEL) // 4)
         pick_ref[...] = flag01(take)
 
     if rounds == 1:
@@ -189,7 +217,7 @@
     every = iota((LANES, 1), 0)
     counts = dot_t(
         flag01(held(grow - (every // 16) * ROWS, gcol - (every % 16) * COLS)),
-        flag01(iota((LANES, 1), 0) == point % HUBS),
+        flag01(iota((LANES, 1), 0) == point_hub),
     )
     overfull[0, 0] = jnp.where(jnp.max(counts) > SLOTS, 1, 0)
 
@@ -344,7 +372,7 @@
                 halves[f // 4] = jnp.where(group == f % 4, folded, halves[f // 4])
             for h in range(HUBS):
                 for half in range(2):
-                    p1send[rnd, turn, h, half * SLOTS : (half + 1) * SLOTS, :] = halves[half][
+                    p1send[rnd, turn, h, half * 4 : half * 4 + SLOTS, :] = halves[half][
                         h * SLOTS : (h + 1) * SLOTS
                     ]
             p1recv[rnd, turn, hub] = p1send[rnd, turn, hub]
@@ -388,69 +416,86 @@
                 hub_sum[...] += turn_sum(turn)
 
             picked = hub_sum[...]
-        for s in range(SEGMENTS):
-            p2send[rnd, s] = picked[2 * s : 2 * s + 2, :]
+        for q in range(SERVED):
+            p2send[rnd, q] = picked[4 * q : 4 * q + 4, :]
         if rnd == 0:
             pl.semaphore_wait(all_in, 1)
 
-        def send(s, kind, to_colat, to_lon):
+        def send(q, kind, to_colat, to_lon):
             pltpu.make_async_remote_copy(
-                src_ref=p2send.at[rnd, s], dst_ref=p2recv.at[rnd, kind, pair * HUBS + hub],
+                src_ref=p2send.at[rnd, q], dst_ref=p2recv.at[rnd, kind, pair * 16 + mix],
                 send_sem=p2_ss.at[rnd], recv_sem=p2_rs.at[rnd, kind],
                 device_id=dict(panel=other, colat=to_colat, lon=to_lon), device_id_type=MESH,
             ).start()
 
-        @pl.loop(0, 16)
-        def _(i):
-            send(i, 0, 0, i)
-            send(16 + i, 1, 7, i)
-
         @pl.loop(0, 8)
         def _(i):
-            send(32 + i, 2, i, 0)
-            send(40 + i, 3, i, 15)
-
-    def place(rnd, ref, base):
+            send(i, 0, 0, 2 * i + 1 - y_lo)
+            send(8 + i, 1, 7, 2 * i + 1 - y_lo)
+
+        for y, kind, to_lon in ((1, 2, 0), (0, 3, 15)):
+
+            @pl.when(y_lo == y)
+            def _():
+                @pl.loop(0, 8)
+                def _(i):
+                    send(16 + i, kind, i, to_lon)
+
+    def make_turns():
         line = iota((64, 1), 0)
-        line_point = line // 2
-        from_row = iota((64, 64), 0)
-        from_col = iota((64, 64), 1)
+        line_point = 16 * ((line // 2) % 2) + line // 4
         for kind, (here, segment) in enumerate(edges):
 
             @pl.when(here)
             def _():
-                wait_bytes(p2recv.at[rnd, kind], p2_rs.at[rnd, kind])
-                total = p2recv[rnd, kind, 0:HUBS]
-                for z in range(1, 4):
-                    total = total + p2recv[rnd, kind, z * HUBS : (z + 1) * HUBS]
-                for h in range(HUBS):
-                    summed[2 * h : 2 * h + 2, :] = total[h]
-                x = summed[...]
                 own = angle[pl.ds(pl.multiple_of((segment // 4) * LANES, LANES), LANES)].reshape(1, LANES)
                 own = jnp.where(lane == (segment % 4) * 32 + line_point, own, 0.0)
                 own = jnp.sum(own, axis=1, keepdims=True)
                 cosine, sine = jnp.cos(own), jnp.sin(own)
-                cosine = jnp.where(group < 2, cosine, 1.0)
-                swap = jnp.where(group == 0, -pltpu.roll(x, 96, 1), pltpu.roll(x, 32, 1))
-                x = cosine * x + jnp.where(group < 2, sine, 0.0) * swap
-                part = from_row // 32
-                at = from_row % 32
-                j = at if kind >= 2 else 4 * (at % 8) + at // 8
-                perm = flag01(from_col == 2 * j + part)
-                x = dot(jnp.concatenate([perm, perm, perm], axis=1), jnp.concatenate(split3(x), axis=0))
+                turn_cos[kind] = jnp.where(group < 2, cosine, 1.0)
+                turn_sin[kind] = jnp.where(group == 0, -sine, jnp.where(group == 1, sine, 0.0))
+
+    def place(rnd, ref, base):
+        for kind, (here, segment) in enumerate(edges):
+
+            @pl.when(here)
+            def _():
+                wait_bytes(p2recv.at[rnd, kind], p2_rs.at[rnd, kind])
+                total = p2recv[rnd, kind, 0:16]
+                for z in range(1, 4):
+                    total = total + p2recv[rnd, kind, z * 16 : (z + 1) * 16]
+                for h in range(16):
+                    summed[4 * h : 4 * h + 4, :] = total[h]
+                x = summed[...]
+                swap = jnp.where(group == 0, pltpu.roll(x, 96, 1), pltpu.roll(x, 32, 1))
+                summed[...] = turn_cos[kind] * x + turn_sin[kind] * swap
+                if kind < 2:
+                    quads = [
+                        [
+                            jnp.concatenate(
+                                [summed[pl.ds(4 * g + 2 * p + half, 4, stride=16), :] for p in range(2)], axis=0
+                            )
+                            for g in range(4)
+                        ]
+                        for half in range(2)
+                    ]
+                else:
+                    columns = [
+                        jnp.concatenate([summed[pl.ds(2 * p + half, 16, stride=4), :] for p in range(2)], axis=0)
+                        for half in range(2)
+                    ]
                 for f in range(7):
-                    block = x[32 * (f // 4) : 32 * (f // 4) + 32]
                     if kind < 2:
                         row = 0 if kind == 0 else ROWS - 1
                         tiles = jnp.zeros((8, LANES), F32)
                         for g in range(4):
-                            moved = pltpu.roll(block[8 * g : 8 * g + 8], 32 * ((g - f % 4) % 4), 1)
+                            moved = pltpu.roll(quads[f // 4][g], 32 * ((g - f % 4) % 4), 1)
                             tiles = jnp.where(group == g, moved, tiles)
                         for t in range(8):
                             ref[f, row : row + 1, base + t * LANES : base + (t + 1) * LANES] = tiles[t : t + 1]
                     else:
                         goal, off = (0, base) if kind == 2 else (3, base + WIDTH - LANES)
-                        moved = pltpu.roll(block, 32 * ((goal - f % 4) % 4), 1)
+                        moved = pltpu.roll(columns[f // 4], 32 * ((goal - f % 4) % 4), 1)
                         now = ref[f, :, off : off + LANES]
                         corner = ((row_id == 0) & (colat == 0)) | ((row_id == ROWS - 1) & (colat == 7))
                         blend = jnp.where(corner, 0.5 * (moved + now), moved)
@@ -460,6 +505,7 @@
         for rnd in range(2):
             ext[rnd, f, :, :LANES] = jnp.zeros((ROWS, LANES), F32)
             ext[rnd, f, :, LANES + WIDTH :] = jnp.zeros((ROWS, LANES), F32)
+    p1send[...] = jnp.zeros(p1send.shape, F32)
     whole_state.wait()
     pack_halo(ext.at[0], LANES, 0)
     pl.semaphore_wait(barrier, 31 + 3 + 1 + 2)
@@ -484,6 +530,7 @@
     for copy in halos1:
         copy.start()
     relay(0)
+    make_turns()
     rate(1, ext.at[0], LANES, out, 0, 0.2)
     for copy in halos1:
         copy.wait_recv()
@@ -510,9 +557,17 @@
             jax.ShapeDtypeStruct((7, ROWS, WIDTH), F32),
             jax.ShapeDtypeStruct((1, 1), I32),
         ),
-        in_specs=[pl.BlockSpec(memory_space=pl.ANY)] + [vmem] * 6,
+        in_specs=[pl.BlockSpec(memory_space=pl.ANY)] * 7,
         out_specs=(vmem, pl.BlockSpec(memory_space=pltpu.SMEM)),
         scratch_shapes=[
+            scratch(1, ROWS, COLS),
+            pltpu.VMEM((4, POINTS), I32),
+            pltpu.VMEM((4, POINTS), I32),
+            pltpu.VMEM((4, POINTS), I32),
+            scratch(4, POINTS),
+            scratch(POINTS),
+            scratch(4, 64, LANES),
+            scratch(4, 64, LANES),
             scratch(2, 7, ROWS, WIDTH + 2 * LANES),
             scratch(2, 2, 8, WIDTH),
             scratch(2, 2, 8, WIDTH),
@@ -520,14 +575,14 @@
             scratch(2, 2, 2, ROWS, LANES),
             scratch(2, rounds, HUBS, PARCEL, LANES),
             scratch(2, rounds, HUBS, PARCEL, LANES),
-            scratch(2, SEGMENTS, 2, LANES),
-            scratch(2, 4, 4 * HUBS, 2, LANES),
+            scratch(2, SERVED, 4, LANES),
+            scratch(2, 4, 64, 4, LANES),
             scratch(64, LANES),
             scratch(HELD, WIDTH),
             scratch(ROWS, WIDTH),
             pltpu.VMEM((HELD, LANES), BF16),
-            pltpu.VMEM((2 * SEGMENTS, HUBS * PARCEL), BF16),
-            scratch(2 * SEGMENTS, LANES),
+            pltpu.VMEM((4 * SERVED, HUBS * PARCEL), BF16),
+            scratch(4 * SERVED, LANES),
             pltpu.SemaphoreType.DMA((2, 4)),
             pltpu.SemaphoreType.DMA((2, 4)),
             pltpu.SemaphoreType.DMA((2, rounds)),
@@ -535,6 +590,7 @@
             pltpu.SemaphoreType.DMA((2,)),
             pltpu.SemaphoreType.DMA((2, 4)),
             pltpu.SemaphoreType.DMA,
+            pltpu.SemaphoreType.DMA((6,)),
             pltpu.SemaphoreType.REGULAR,
             pltpu.SemaphoreType.REGULAR,
         ],
@@ -548,7 +604,7 @@
 def on_device(state, spin, donor_device, donor_row, donor_col, corner_weights, border_angle):
     args = (state[0], spin, donor_device, donor_row, donor_col, corner_weights, border_angle)
     fast, overfull = step(1, *args)
-    turns = POINTS // HUBS // SLOTS
+    turns = -(-POINTS // (HUBS * SLOTS))
     advanced = lax.cond(overfull[0, 0] > 0, lambda: step(turns, *args)[0], lambda: fast)
     return advanced[None]
 

time: 44.9 us -> 43.2 us (0.962)
  Pallas kernels: 43 us -> 41.3 us
    pallas_call x1, Pallas kernels: 43 us -> 41.3 us  [step(): pl.pallas_call(functools.partial(step_kernel, rounds), out_shape=(jax.Sha...]
where the time goes in v5:
time: 43.2 us; the launch traced here: 43 us
  Pallas kernels  41.3 us (96%)
  local copies, waits for them, and re-layouts  0.95 us (2%)
  between operations  0.74 us (2%)
    pallas_call x1, Pallas kernels, step(): pl.pallas_call(functools.partial(step_kernel, rounds), out_shape=(jax.Sha...  41.3 us
    unnamed x15, local copies, waits for them, and re-layouts  0.95 us

profile of v5, /device:TPU:1, one launch (start us, length us, event | category | flops | bytes accessed | tf_op | source)
XLA Modules:
  0.0 43.0 jit_solution(9640255250916025249)
XLA Ops:
  0.0 0.0 copy-start
  0.0 0.0 copy-start.1
  0.0 0.0 copy-start.2
  0.0 0.0 copy-start.3
  0.0 0.0 copy-start.4
  0.0 0.0 copy-start.5
  0.0 0.0 copy-start.6
  0.0 41.3 %dynamo_step.1 = (f32[7,32,1024]{2,1,0:T(8,128)S(1)}, s32[1,1]{1,0:T(1,128)}) custom-call(f32[7,32,1024]{2,1,0:T(8,128)} %bitcast.4, f32[1,32,32]{2,1,0:T(8,128)} %spin_in.1, s32[4,1536]{1,0:T(4,128)} %device_in.1, s32[4,1536]{1,0:T(4,128)} %drow_in.1, s32[4,1536]{1,0:T(4,128)} %dcol_in.1, f32[4,1536]{1,0:T(4,128)} %weights_in.1, f32[1536]{0:T(1024)} %angle_in.1), custom_call_target="tpu_custom_call" | custom-call | tf_op jit(solution)/shard_map/dynamo_step/pallas_call | solution.py:554
  42.0 0.0 copy-done
  42.0 0.0 copy-done.1
  42.0 0.0 copy-done.2
  42.1 0.0 copy-done.3
  42.1 0.0 copy-done.4
  42.1 0.0 copy-done.5
  42.1 0.0 copy-done.6
  42.1 0.9 %copy.14 = f32[1,7,32,1024]{3,2,1,0:T(8,128)} copy(f32[1,7,32,1024]{3,2,1,0:T(8,128)S(1)} %get-tuple-element.37) | data formatting | bytes 1835008
  (1 shorter events, 0.0 us)
Async XLA Ops:
  0.0 42.0 %copy-start = (f32[1,7,32,1024]{3,2,1,0:T(8,128)S(1)}, f32[1,7,32,1024]{3,2,1,0:T(8,128)}, u32[]{:S(2)}) copy-start(f32[1,7,32,1024]{3,2,1,0:T(8,128)} %param.9) | copy-start | bytes 2752516
  0.0 42.0 %copy-start.1 = (s32[4,1536]{1,0:T(4,128)S(1)}, s32[4,1536]{1,0:T(4,128)}, u32[]{:S(2)}) copy-start(s32[4,1536]{1,0:T(4,128)} %device_in.1) | copy-start | bytes 73732
  0.0 42.0 %copy-start.2 = (s32[4,1536]{1,0:T(4,128)S(1)}, s32[4,1536]{1,0:T(4,128)}, u32[]{:S(2)}) copy-start(s32[4,1536]{1,0:T(4,128)} %drow_in.1) | copy-start | bytes 73732
  0.0 42.1 %copy-start.3 = (s32[4,1536]{1,0:T(4,128)S(1)}, s32[4,1536]{1,0:T(4,128)}, u32[]{:S(2)}) copy-start(s32[4,1536]{1,0:T(4,128)} %dcol_in.1) | copy-start | bytes 73732
  0.0 42.1 %copy-start.4 = (f32[4,1536]{1,0:T(4,128)S(1)}, f32[4,1536]{1,0:T(4,128)}, u32[]{:S(2)}) copy-start(f32[4,1536]{1,0:T(4,128)} %weights_in.1) | copy-start | bytes 73732
  0.0 42.1 %copy-start.5 = (f32[1,32,32]{2,1,0:T(8,128)S(1)}, f32[1,32,32]{2,1,0:T(8,128)}, u32[]{:S(2)}) copy-start(f32[1,32,32]{2,1,0:T(8,128)} %spin_in.1) | copy-start | bytes 12292
  0.0 42.1 %copy-start.6 = (f32[1536]{0:T(1024)S(1)}, f32[1536]{0:T(1024)}, u32[]{:S(2)}) copy-start(f32[1536]{0:T(1024)} %angle_in.1) | copy-start | bytes 18436

commit v6 on v5

--- a/solution.py
+++ b/solution.py
@@ -13,6 +13,10 @@
 POINTS, HUBS, SLOTS, PARCEL = 1536, 32, 3, 8
 HELD = HUBS * SLOTS
 SERVED = 24
+PEERS = sorted(
+    [(c, k, y, o) for c in range(4) for k in range(2) for y in range(2) for o in range(2) if c or k or y or o],
+    key=lambda s: -(min(s[0], 4 - s[0]) + s[2] + s[3]),
+)
 DIFFUSE = (0.3, 0.3, 0.3, 0.4, 0.5, 0.5, 0.5)
 
 
@@ -64,6 +68,11 @@
 
     def peer(h):
         return dict(colat=(h % 16) // 2, lon=(pair * 2 + h % 2) * 2 + h // 16)
+
+    def peer_hub(step):
+        chip, core, side_step, odd_step = step
+        to_colat = ((colat // 2 + chip) % 4) * 2 + (colat + core) % 2
+        return ((y_lo + side_step) % 2) * 16 + to_colat * 2 + (odd + odd_step) % 2
 
     def across(f):
         return dict(lon=(((pair + f) % 4) * 2 + odd) * 2 + y_lo)
@@ -85,9 +94,8 @@
     for copy in tables[4:]:
         copy.start()
 
-    @pl.loop(1, HUBS)
-    def _(f):
-        greet(**peer((hub + f) % HUBS))
+    for step in PEERS:
+        greet(**peer(peer_hub(step)))
 
     @pl.loop(1, 4)
     def _(f):
@@ -305,7 +313,7 @@
             place_at = (f, slice(None), slice(dst_off + t * LANES, dst_off + (t + 1) * LANES))
             dst[place_at] += change
 
-    def add_halos(rnd, dst, dst_off, dt):
+    def add_halos(rnd, copies, dst, dst_off, dt):
         def recv_row(side):
             return lambda t: rowrecv[rnd, side, :, t * LANES : (t + 1) * LANES]
 
@@ -316,8 +324,12 @@
 
             return values
 
+        for copy in copies[:2]:
+            copy.wait_recv()
         pl.when(colat > 0)(lambda: add_row(rnd, dst, dst_off, dt, 0, -1.0, recv_row(0)))
         pl.when(colat < 7)(lambda: add_row(rnd, dst, dst_off, dt, ROWS - 1, 1.0, recv_row(1)))
+        for copy in copies[2:]:
+            copy.wait_recv()
         pl.when(lon > 0)(lambda: add_col(rnd, dst, dst_off, dt, 0, -1.0, recv_col(0, 0)))
         pl.when(lon < 15)(lambda: add_col(rnd, dst, dst_off, dt, 7, 1.0, recv_col(1, 3)))
 
@@ -359,7 +371,7 @@
 
     def send_points(ref, base, rnd):
         def turn_points(turn):
-            halves = [jnp.zeros((HELD, LANES), F32) for _ in range(2)]
+            found = []
             lhs = lhs_ref[...][:, :96]
             for f in range(7):
                 hi, lo = split2(ref[f, :, base : base + WIDTH])
@@ -367,9 +379,15 @@
                 folded = jnp.zeros((HELD, LANES), F32)
                 for t in range(8):
                     folded += rows[:, t * LANES : (t + 1) * LANES] * spread[:, t * LANES : (t + 1) * LANES]
-                folded += pltpu.roll(folded, 32, 1)
-                folded += pltpu.roll(folded, 64, 1)
-                halves[f // 4] = jnp.where(group == f % 4, folded, halves[f // 4])
+                found.append(folded)
+            even, left = group % 2 == 0, group < 2
+
+            def fold(a, b, c, d):
+                ab = jnp.where(even, a, b) + pltpu.roll(jnp.where(even, b, a), 96, 1)
+                cd = jnp.where(even, c, d) + pltpu.roll(jnp.where(even, d, c), 96, 1)
+                return jnp.where(left, ab, cd) + pltpu.roll(jnp.where(left, cd, ab), 64, 1)
+
+            halves = [fold(*found[:4]), fold(*found[4:], found[6])]
             for h in range(HUBS):
                 for half in range(2):
                     p1send[rnd, turn, h, half * 4 : half * 4 + SLOTS, :] = halves[half][
@@ -377,9 +395,8 @@
                     ]
             p1recv[rnd, turn, hub] = p1send[rnd, turn, hub]
 
-            @pl.loop(1, HUBS)
-            def _(f):
-                h = (hub + f) % HUBS
+            for step in PEERS:
+                h = peer_hub(step)
                 pltpu.make_async_remote_copy(
                     src_ref=p1send.at[rnd, turn, h], dst_ref=p1recv.at[rnd, turn, hub],
                     send_sem=p1_ss.at[rnd, turn], recv_sem=p1_rs.at[rnd, turn],
@@ -428,8 +445,7 @@
                 device_id=dict(panel=other, colat=to_colat, lon=to_lon), device_id_type=MESH,
             ).start()
 
-        @pl.loop(0, 8)
-        def _(i):
+        for i in range(8):
             send(i, 0, 0, 2 * i + 1 - y_lo)
             send(8 + i, 1, 7, 2 * i + 1 - y_lo)
 
@@ -437,8 +453,7 @@
 
             @pl.when(y_lo == y)
             def _():
-                @pl.loop(0, 8)
-                def _(i):
+                for i in range(8):
                     send(16 + i, kind, i, to_lon)
 
     def make_turns():
@@ -518,9 +533,7 @@
         pl.semaphore_signal(ready, inc=1, device_id=across(f), device_id_type=MESH)
 
     rate(0, ext.at[0], LANES, ext.at[1], LANES, 0.1)
-    for copy in halos0:
-        copy.wait_recv()
-    add_halos(0, ext.at[1], LANES, 0.1)
+    add_halos(0, halos0, ext.at[1], LANES, 0.1)
     clear_border(ext.at[1], LANES)
     send_points(ext.at[1], LANES, 0)
     pl.semaphore_wait(ready, 3)
@@ -532,9 +545,7 @@
     relay(0)
     make_turns()
     rate(1, ext.at[0], LANES, out, 0, 0.2)
-    for copy in halos1:
-        copy.wait_recv()
-    add_halos(1, out, 0, 0.2)
+    add_halos(1, halos1, out, 0, 0.2)
     place(0, ext.at[1], LANES)
     add_border(out, 0, 0.2)
     send_points(out, 0, 1)
@@ -605,7 +616,7 @@
     args = (state[0], spin, donor_device, donor_row, donor_col, corner_weights, border_angle)
     fast, overfull = step(1, *args)
     turns = -(-POINTS // (HUBS * SLOTS))
-    advanced = lax.cond(overfull[0, 0] > 0, lambda: step(turns, *args)[0], lambda: fast)
+    advanced = lax.switch(overfull[0, 0], [lambda: fast, lambda: step(turns, *args)[0]])
     return advanced[None]
 
 

time: 43.2 us -> 41.9 us (0.970)
  Pallas kernels: 41.3 us -> 40.1 us
    pallas_call x1, Pallas kernels: 41.3 us -> 40.1 us  [step(): pl.pallas_call(functools.partial(step_kernel, rounds), out_shape=(jax.Sha...]
where the time goes in v6:
time: 41.9 us; the launch traced here: 41.8 us
  Pallas kernels  40.1 us (96%)
  local copies, waits for them, and re-layouts  0.95 us (2%)
  between operations  0.74 us (2%)
    pallas_call x1, Pallas kernels, step(): pl.pallas_call(functools.partial(step_kernel, rounds), out_shape=(jax.Sha...  40.1 us
    unnamed x15, local copies, waits for them, and re-layouts  0.95 us

profile of v6, /device:TPU:1, one launch (start us, length us, event | category | flops | bytes accessed | tf_op | source)
XLA Modules:
  0.0 41.8 jit_solution(16349120500616532616)
XLA Ops:
  0.0 0.0 copy-start
  0.0 0.0 copy-start.1
  0.0 0.0 copy-start.2
  0.0 0.0 copy-start.3
  0.0 0.0 copy-start.4
  0.0 0.0 copy-start.5
  0.0 0.0 copy-start.6
  0.0 40.1 %dynamo_step.1 = (f32[7,32,1024]{2,1,0:T(8,128)S(1)}, s32[1,1]{1,0:T(1,128)}) custom-call(f32[7,32,1024]{2,1,0:T(8,128)} %bitcast.4, f32[1,32,32]{2,1,0:T(8,128)} %spin_in.1, s32[4,1536]{1,0:T(4,128)} %device_in.1, s32[4,1536]{1,0:T(4,128)} %drow_in.1, s32[4,1536]{1,0:T(4,128)} %dcol_in.1, f32[4,1536]{1,0:T(4,128)} %weights_in.1, f32[1536]{0:T(1024)} %angle_in.1), custom_call_target="tpu_custom_call" | custom-call | tf_op jit(solution)/shard_map/dynamo_step/pallas_call | solution.py:565
  40.8 0.0 copy-done
  40.8 0.0 copy-done.1
  40.8 0.0 copy-done.2
  40.8 0.0 copy-done.3
  40.8 0.0 copy-done.4
  40.8 0.0 copy-done.5
  40.8 0.0 copy-done.6
  40.9 0.9 %copy.14 = f32[1,7,32,1024]{3,2,1,0:T(8,128)} copy(f32[1,7,32,1024]{3,2,1,0:T(8,128)S(1)} %get-tuple-element.37) | data formatting | bytes 1835008
  (1 shorter events, 0.0 us)
Async XLA Ops:
  0.0 40.8 %copy-start = (f32[1,7,32,1024]{3,2,1,0:T(8,128)S(1)}, f32[1,7,32,1024]{3,2,1,0:T(8,128)}, u32[]{:S(2)}) copy-start(f32[1,7,32,1024]{3,2,1,0:T(8,128)} %param.9) | copy-start | bytes 2752516
  0.0 40.8 %copy-start.1 = (s32[4,1536]{1,0:T(4,128)S(1)}, s32[4,1536]{1,0:T(4,128)}, u32[]{:S(2)}) copy-start(s32[4,1536]{1,0:T(4,128)} %device_in.1) | copy-start | bytes 73732
  0.0 40.8 %copy-start.2 = (s32[4,1536]{1,0:T(4,128)S(1)}, s32[4,1536]{1,0:T(4,128)}, u32[]{:S(2)}) copy-start(s32[4,1536]{1,0:T(4,128)} %drow_in.1) | copy-start | bytes 73732
  0.0 40.8 %copy-start.3 = (s32[4,1536]{1,0:T(4,128)S(1)}, s32[4,1536]{1,0:T(4,128)}, u32[]{:S(2)}) copy-start(s32[4,1536]{1,0:T(4,128)} %dcol_in.1) | copy-start | bytes 73732
  0.0 40.8 %copy-start.4 = (f32[4,1536]{1,0:T(4,128)S(1)}, f32[4,1536]{1,0:T(4,128)}, u32[]{:S(2)}) copy-start(f32[4,1536]{1,0:T(4,128)} %weights_in.1) | copy-start | bytes 73732
  0.0 40.8 %copy-start.5 = (f32[1,32,32]{2,1,0:T(8,128)S(1)}, f32[1,32,32]{2,1,0:T(8,128)}, u32[]{:S(2)}) copy-start(f32[1,32,32]{2,1,0:T(8,128)} %spin_in.1) | copy-start | bytes 12292
  0.0 40.8 %copy-start.6 = (f32[1536]{0:T(1024)S(1)}, f32[1536]{0:T(1024)}, u32[]{:S(2)}) copy-start(f32[1536]{0:T(1024)} %angle_in.1) | copy-start | bytes 18436

commit v7 on v6

--- a/solution.py
+++ b/solution.py
@@ -97,10 +97,8 @@
     for step in PEERS:
         greet(**peer(peer_hub(step)))
 
-    @pl.loop(1, 4)
-    def _(f):
+    for f in (2, 1, 3):
         greet(**across(f))
-
     greet(panel=other)
     north, south = (colat + 7) % 8, (colat + 1) % 8
     west, east = (lon + 15) % 16, (lon + 1) % 16
@@ -375,10 +373,11 @@
             lhs = lhs_ref[...][:, :96]
             for f in range(7):
                 hi, lo = split2(ref[f, :, base : base + WIDTH])
-                rows = dot(lhs, jnp.concatenate([hi, hi, lo], axis=0))
+                stacked = jnp.concatenate([hi, hi, lo], axis=0)
                 folded = jnp.zeros((HELD, LANES), F32)
-                for t in range(8):
-                    folded += rows[:, t * LANES : (t + 1) * LANES] * spread[:, t * LANES : (t + 1) * LANES]
+                for t in range(0, 8, 2):
+                    rows = dot(lhs, stacked[:, t * LANES : (t + 2) * LANES]) * spread[:, t * LANES : (t + 2) * LANES]
+                    folded += rows[:, :LANES] + rows[:, LANES:]
                 found.append(folded)
             even, left = group % 2 == 0, group < 2
 
@@ -445,7 +444,8 @@
                 device_id=dict(panel=other, colat=to_colat, lon=to_lon), device_id_type=MESH,
             ).start()
 
-        for i in range(8):
+        for away in (4, 3, 5, 2, 6, 1, 7, 0):
+            i = (plane + away) % 8
             send(i, 0, 0, 2 * i + 1 - y_lo)
             send(8 + i, 1, 7, 2 * i + 1 - y_lo)
 
@@ -525,11 +525,10 @@
     pack_halo(ext.at[0], LANES, 0)
     pl.semaphore_wait(barrier, 31 + 3 + 1 + 2)
     halos0 = halo_copies(0)
-    for copy in halos0:
+    for copy in halos0[2:] + halos0[:2]:
         copy.start()
 
-    @pl.loop(1, 4)
-    def _(f):
+    for f in (2, 1, 3):
         pl.semaphore_signal(ready, inc=1, device_id=across(f), device_id_type=MESH)
 
     rate(0, ext.at[0], LANES, ext.at[1], LANES, 0.1)

time: 41.9 us -> 41.7 us (level)
  no operation moved by 1% of the time
where the time goes in v7:
time: 41.7 us; the launch traced here: 41.6 us
  Pallas kernels  39.9 us (96%)
  local copies, waits for them, and re-layouts  0.95 us (2%)
  between operations  0.74 us (2%)
    pallas_call x1, Pallas kernels, step(): pl.pallas_call(functools.partial(step_kernel, rounds), out_shape=(jax.Sha...  39.9 us
    unnamed x15, local copies, waits for them, and re-layouts  0.95 us

profile of v7, /device:TPU:1, one launch (start us, length us, event | category | flops | bytes accessed | tf_op | source)
XLA Modules:
  0.0 41.6 jit_solution(15766971668747990960)
XLA Ops:
  0.0 0.0 copy-start
  0.0 0.0 copy-start.1
  0.0 0.0 copy-start.2
  0.0 0.0 copy-start.3
  0.0 0.0 copy-start.4
  0.0 0.0 copy-start.5
  0.0 0.0 copy-start.6
  0.0 39.9 %dynamo_step.1 = (f32[7,32,1024]{2,1,0:T(8,128)S(1)}, s32[1,1]{1,0:T(1,128)}) custom-call(f32[7,32,1024]{2,1,0:T(8,128)} %bitcast.4, f32[1,32,32]{2,1,0:T(8,128)} %spin_in.1, s32[4,1536]{1,0:T(4,128)} %device_in.1, s32[4,1536]{1,0:T(4,128)} %drow_in.1, s32[4,1536]{1,0:T(4,128)} %dcol_in.1, f32[4,1536]{1,0:T(4,128)} %weights_in.1, f32[1536]{0:T(1024)} %angle_in.1), custom_call_target="tpu_custom_call" | custom-call | tf_op jit(solution)/shard_map/dynamo_step/pallas_call | solution.py:564
  40.6 0.0 copy-done
  40.6 0.0 copy-done.1
  40.6 0.0 copy-done.2
  40.6 0.0 copy-done.3
  40.7 0.0 copy-done.4
  40.7 0.0 copy-done.5
  40.7 0.0 copy-done.6
  40.7 0.9 %copy.14 = f32[1,7,32,1024]{3,2,1,0:T(8,128)} copy(f32[1,7,32,1024]{3,2,1,0:T(8,128)S(1)} %get-tuple-element.37) | data formatting | bytes 1835008
  (1 shorter events, 0.0 us)
Async XLA Ops:
  0.0 40.6 %copy-start = (f32[1,7,32,1024]{3,2,1,0:T(8,128)S(1)}, f32[1,7,32,1024]{3,2,1,0:T(8,128)}, u32[]{:S(2)}) copy-start(f32[1,7,32,1024]{3,2,1,0:T(8,128)} %param.9) | copy-start | bytes 2752516
  0.0 40.6 %copy-start.1 = (s32[4,1536]{1,0:T(4,128)S(1)}, s32[4,1536]{1,0:T(4,128)}, u32[]{:S(2)}) copy-start(s32[4,1536]{1,0:T(4,128)} %device_in.1) | copy-start | bytes 73732
  0.0 40.6 %copy-start.2 = (s32[4,1536]{1,0:T(4,128)S(1)}, s32[4,1536]{1,0:T(4,128)}, u32[]{:S(2)}) copy-start(s32[4,1536]{1,0:T(4,128)} %drow_in.1) | copy-start | bytes 73732
  0.0 40.6 %copy-start.3 = (s32[4,1536]{1,0:T(4,128)S(1)}, s32[4,1536]{1,0:T(4,128)}, u32[]{:S(2)}) copy-start(s32[4,1536]{1,0:T(4,128)} %dcol_in.1) | copy-start | bytes 73732
  0.0 40.6 %copy-start.4 = (f32[4,1536]{1,0:T(4,128)S(1)}, f32[4,1536]{1,0:T(4,128)}, u32[]{:S(2)}) copy-start(f32[4,1536]{1,0:T(4,128)} %weights_in.1) | copy-start | bytes 73732
  0.0 40.6 %copy-start.5 = (f32[1,32,32]{2,1,0:T(8,128)S(1)}, f32[1,32,32]{2,1,0:T(8,128)}, u32[]{:S(2)}) copy-start(f32[1,32,32]{2,1,0:T(8,128)} %spin_in.1) | copy-start | bytes 12292
  0.0 40.6 %copy-start.6 = (f32[1536]{0:T(1024)S(1)}, f32[1536]{0:T(1024)}, u32[]{:S(2)}) copy-start(f32[1536]{0:T(1024)} %angle_in.1) | copy-start | bytes 18436
